TPU v7x, 32 devices: a whole 2x2x4 slice. The times are simulated.
32 devices in a mesh: grp: 2 (over x), seq: 8 (over z, y), chan: 2 (over core).
Axes of the slice: x: 2, y: 2, z: 4, core: 2. Of those that a mesh axis runs over, the one named last changes fastest.
Arguments:
- inputs: bfloat16 [262144, 768], P(('grp', 'seq'), 'chan'), parts along dimension 0, may hold values from -6 to 6
- cotangent: bfloat16 [262144, 768], P(('grp', 'seq'), 'chan'), parts along dimension 0, may hold values from -6 to 6
- conv_weight: float32 [2, 4, 768], P(None, None, 'chan'), may hold values from -3 to 3
- mix_inner: bfloat16 [256, 256], replicated, may hold values from -0.375 to 0.375
- twiddle: float32 [512, 256], P('seq'), may hold values from 0.5 to 2
- mix_outer: bfloat16 [512, 512], replicated, may hold values from -0.25 to 0.25
- proj_weight: bfloat16 [768, 768], P(None, 'chan'), may hold values from -0.21875 to 0.21875
Outputs:
- input_grad: bfloat16 [262144, 768], P(('grp', 'seq'), 'chan'), parts along dimension 0
- proj_grad: bfloat16 [1536, 768], P('grp', 'chan'), parts along dimension 0
- inner_grad: float32 [512, 256], P('grp'), parts along dimension 0
- outer_grad: float32 [1024, 512], P('grp'), parts along dimension 0
- conv_grad: float32 [4, 4, 768], P('grp', None, 'chan'), parts along dimension 0
There are 2 independent parts, one for each index of `grp`. A program takes and returns all parts, laid end to end along the dimension named above; an argument that names none is the same for every part. Nothing has to cross between parts.
All inputs are finite; a program needn't handle non-finite values.
Results may differ from a plain program's by a relative error of at most 0.0067.
Values may be sent and summed in bfloat16 or wider, within the bound.
A program may use at most 448 MiB of HBM per device.

v0:
```python
import jax
import jax.numpy as jnp
from jax import lax
from jax.sharding import PartitionSpec as P


def passed_along(array, axis, by):
    peers = lax.axis_size(axis)
    pairs = [(i, i + by) for i in range(peers) if 0 <= i + by < peers]
    return lax.ppermute(array, axis, pairs)


def causal_taps(history_rows, weights, tokens):
    result = weights[0] * history_rows[3 : 3 + tokens]
    for offset in range(1, 4):
        result = result + weights[offset] * history_rows[3 - offset : 3 - offset + tokens]
    return result


def taps_ahead(extended, weights, tokens):
    result = weights[0] * extended[0:tokens]
    for offset in range(1, 4):
        result = result + weights[offset] * extended[offset : offset + tokens]
    return result


def taps_grad(signal, history_rows, tokens):
    totals = []
    for offset in range(4):
        totals.append(jnp.sum(signal * history_rows[3 - offset : 3 - offset + tokens], 0))
    return jnp.stack(totals)


def body(inputs, cotangent, conv_weight, mix_inner, twiddle, mix_outer, proj_weight):
    inner_size = mix_inner.shape[0]
    tokens, channels = inputs.shape
    blocks = tokens // inner_size
    grad_scale = (mix_outer.shape[0] * inner_size) ** (-0.5)
    last_rows = passed_along(inputs[tokens - 3 :], "seq", 1)
    history_rows = jnp.concatenate([last_rows, inputs], 0).astype(jnp.float32)
    value_conv = causal_taps(history_rows, conv_weight[0], tokens)
    gate_conv = causal_taps(history_rows, conv_weight[1], tokens)
    gate_sig = jax.nn.sigmoid(gate_conv)
    gated_input = (value_conv * gate_sig).astype(jnp.bfloat16)
    gated_blocks = gated_input.reshape(blocks, inner_size, channels)
    inner_mixed = jnp.einsum(
        "kj,ijc->ikc", mix_inner, gated_blocks, preferred_element_type=jnp.float32
    )
    twisted = (inner_mixed * twiddle[:, :, None]).astype(jnp.bfloat16)
    received = lax.all_to_all(twisted, "seq", split_axis=1, concat_axis=0, tiled=True)
    product = jnp.einsum("mi,ikc->mkc", mix_outer, received, preferred_element_type=jnp.float32)
    mixed_turned = product.astype(jnp.bfloat16)
    cotangent_turned = lax.all_to_all(
        cotangent.reshape(blocks, inner_size, channels),
        "seq",
        split_axis=1,
        concat_axis=0,
        tiled=True,
    )
    mixed_rows = mixed_turned.reshape(-1, channels)
    grad_rows = cotangent_turned.reshape(-1, channels)
    proj_part = lax.dot_general(
        lax.all_gather(mixed_rows, "chan", axis=1, tiled=True),
        grad_rows,
        (((0,), (0,)), ((), ())),
        preferred_element_type=jnp.float32,
    )
    full_terms = lax.dot_general(
        grad_rows, proj_weight, (((1,), (1,)), ((), ())), preferred_element_type=jnp.float32
    )
    mixed_grad = lax.psum_scatter(full_terms, "chan", scatter_dimension=1, tiled=True)
    mixed_grad = mixed_grad.astype(jnp.bfloat16)
    grad_turned = mixed_grad.reshape(mixed_turned.shape)
    outer_part = jnp.einsum(
        "mkc,ikc->mi", grad_turned, received, preferred_element_type=jnp.float32
    )
    twisted_grad_turned = jnp.einsum(
        "mi,mkc->ikc", mix_outer, grad_turned, preferred_element_type=jnp.float32
    ).astype(jnp.bfloat16)
    twisted_grad = lax.all_to_all(
        twisted_grad_turned, "seq", split_axis=0, concat_axis=1, tiled=True
    )
    inner_mixed_grad = (twisted_grad.astype(jnp.float32) * twiddle[:, :, None]).astype(jnp.bfloat16)
    gated_grad = jnp.einsum(
        "kj,ikc->ijc", mix_inner, inner_mixed_grad, preferred_element_type=jnp.float32
    ).reshape(tokens, channels)
    inner_part = jnp.einsum(
        "ikc,ijc->kj", inner_mixed_grad, gated_blocks, preferred_element_type=jnp.float32
    )
    value_grad = gated_grad * gate_sig
    gate_grad = gated_grad * value_conv * gate_sig * (1.0 - gate_sig)
    next_value, next_gate = passed_along((value_grad[:3], gate_grad[:3]), "seq", -1)
    value_extended = jnp.concatenate([value_grad, next_value], 0)
    gate_extended = jnp.concatenate([gate_grad, next_gate], 0)
    input_grad = (
        cotangent.astype(jnp.float32)
        + taps_ahead(value_extended, conv_weight[0], tokens)
        + taps_ahead(gate_extended, conv_weight[1], tokens)
    )
    conv_part = jnp.stack(
        [taps_grad(value_grad, history_rows, tokens), taps_grad(gate_grad, history_rows, tokens)]
    )
    proj_sum, conv_sum = lax.psum((proj_part, conv_part), "seq")
    inner_sum, outer_sum = lax.psum((inner_part, outer_part), ("seq", "chan"))
    return (
        input_grad.astype(jnp.bfloat16),
        (proj_sum * grad_scale).astype(jnp.bfloat16),
        inner_sum * grad_scale,
        outer_sum * grad_scale,
        conv_sum * grad_scale,
    )


def solution(mesh):
    in_specs = (
        P(("grp", "seq"), "chan"),
        P(("grp", "seq"), "chan"),
        P(None, None, "chan"),
        P(),
        P("seq", None),
        P(),
        P(None, "chan"),
    )
    out_specs = (
        P(("grp", "seq"), "chan"),
        P("grp", "chan"),
        P("grp", None),
        P("grp", None),
        P("grp", None, "chan"),
    )
    return jax.shard_map(body, mesh=mesh, in_specs=in_specs, out_specs=out_specs, check_vma=False)
```

profile of v0, /device:TPU:0, one launch (start us, length us, event | category | flops | bytes accessed | tf_op | source)
XLA Modules:
  0.0 1524.8 jit_solution(11186363642366659747)
XLA Ops:
  7.2 0.0 copy-start
  7.2 0.0 reduce-scatter.2.cloned.1.call-start
  7.2 11.6 copy.55
  18.8 280.0 %all_to_all.42 = bf16[64,256,384]{2,0,1:T(8,128)(2,1)S(1)} all-to-all(bf16[64,256,384]{2,0,1:T(8,128)(2,1)S(1)} %copy.55), channel_id=1, replica_groups=mesh['grp'=2,'seq'=8,'chan'=2] {'seq'}, dimensions={1} | all-to-all | bytes 25165824 | tf_op jit(solution)/shard_map/all_to_all | solution.py:53
  298.8 9.3 copy.57
  308.2 0.0 copy-done
  308.2 25.5 %fusion.45 = f32[16384,768]{1,0:T(8,128)} fusion(bf16[16384,384]{1,0:T(8,128)(2,1)} %bitcast.66, bf16[768,384]{1,0:T(8,128)(2,1)S(1)} %copy-done), kind=kOutput, calls=%fused_computation.77 | convolution fusion | flops 9663676416 | bytes 63504384 | tf_op jit(solution)/shard_map/dot_general | solution.py:68
  333.7 0.0 reduce-scatter.2.cloned.1.call-update
  333.7 0.0 copy-start.6
  333.7 62.5 %reduce-scatter.2.cloned.1.call-done = f32[16384,384]{1,0:T(8,128)} async-done(((f32[16384,768]{1,0:T(8,128)}), f32[16384,384]{1,0:T(8,128)}) %reduce-scatter.2.cloned.1.call-update) | async-done | bytes 25165840 | tf_op jit(solution)/shard_map/reduce_scatter | solution.py:71
  396.2 13.2 convert_element_type.52
  409.5 0.0 copy-done.6
  409.5 33.4 %convert_bitcast_fusion.2 = bf16[512,32,384]{0,2,1:T(8,128)(2,1)} fusion(bf16[512,32,384]{2,1,0:T(8,128)(2,1)} %bitcast.74, bf16[512,512]{1,0:T(8,128)(2,1)S(1)} %copy-done.6), kind=kOutput, calls=%fused_computation.47 | convolution fusion | flops 6448742400 | bytes 25690112 | tf_op jit(solution)/shard_map/mi,mkc->ikc/dot_general | solution.py:77
  442.9 0.0 copy-start.5
  443.0 16.7 %copy.59 = bf16[512,32,384]{2,1,0:T(8,128)(2,1)} copy(bf16[512,32,384]{0,2,1:T(8,128)(2,1)} %convert_bitcast_fusion.2) | data formatting | bytes 25165824 | tf_op jit(solution)/shard_map/convert_element_type | solution.py:79
  459.7 5.7 all-to-all-start.1
  465.4 0.0 all-gather.2.cloned.1.call-start
  465.5 0.7 slice.105
  466.2 3.9 collective-permute-start
  470.1 0.0 copy-done.5
  470.1 97.2 %collective-permute-done = bf16[3,384]{1,0:T(4,128)(2,1)S(1)} collective-permute-done((bf16[3,384]{1,0:T(4,128)(2,1)S(1)}, bf16[3,384]{1,0:T(4,128)(2,1)S(1)}, u32[]{:S(2)}, u32[]{:S(2)}) %collective-permute-start) | collective-permute-done | bytes 2336 | tf_op jit(solution)/shard_map/ppermute | solution.py:10
  567.3 14.2 maximum_convert_fusion
  581.5 157.5 %all-to-all-done.1 = bf16[512,32,384]{2,1,0:T(8,128)(2,1)} async-done(((bf16[512,32,384]{2,1,0:T(8,128)(2,1)}), bf16[512,32,384]{2,1,0:T(8,128)(2,1)}, u32[]{:S(2)}, u32[]{:S(2)}) %all-to-all-start.1) | async-done | bytes 12582944 | tf_op jit(solution)/shard_map/all_to_all | solution.py:80
  739.0 7.5 convert_bitcast_fusion
  746.5 0.0 copy-start.3
  746.5 9.6 copy.60
  756.1 0.0 copy-done.3
  756.1 9.9 fusion.21
  766.1 0.0 copy-done.4
  766.1 0.0 copy-start.2
  766.1 10.6 fusion.42
  776.6 1.4 copy-done.2
  778.0 79.5 %multiply_reduce_fusion.7 = (f32[384]{0:T(512)S(1)}, f32[384]{0:T(512)S(1)}, f32[384]{0:T(512)S(1)}, f32[384]{0:T(512)S(1)}, f32[384]{0:T(512)S(1)}, /*index=5*/...) fusion(f32[16387,384]{1,0:T(8,128)} %maximum_convert_fusion, ...), kind=kLoop, calls=%fused_computation.39 | loop fusion | flops 239072256 | bytes 226516992 | tf_op jit(solution)/shard_map/reduce_sum | solution.py:30
  857.6 21.3 %multiply_convert_fusion.1 = bf16[16384,384]{1,0:T(8,128)(2,1)} fusion(f32[16384,384]{1,0:T(8,128)} %get-tuple-element.29, f32[16384,384]{1,0:T(8,128)} %get-tuple-element.30), kind=kLoop, calls=%fused_computation.41 | loop fusion | flops 12582912 | bytes 62914560 | tf_op jit(solution)/shard_map/convert_element_type | solution.py:44
  878.9 12.5 fusion.22
  891.5 16.8 %copy.63 = bf16[64,256,384]{2,0,1:T(8,128)(2,1)} copy(bf16[64,256,384]{1,2,0:T(8,128)(2,1)} %fusion.22) | data formatting | bytes 25165824 | tf_op jit(solution)/shard_map/convert_element_type | solution.py:49
  908.3 290.3 %all_to_all.43 = bf16[64,256,384]{2,0,1:T(8,128)(2,1)S(1)} all-to-all(bf16[64,256,384]{2,0,1:T(8,128)(2,1)} %copy.63), channel_id=1, replica_groups=mesh['grp'=2,'seq'=8,'chan'=2] {'seq'}, dimensions={1} | all-to-all | bytes 25165824 | tf_op jit(solution)/shard_map/all_to_all | solution.py:50
  1198.6 9.5 copy.65
  1208.1 32.2 %convert_bitcast_fusion.1 = bf16[512,32,384]{0,2,1:T(8,128)(2,1)} fusion(bf16[512,32,384]{2,1,0:T(8,128)(2,1)} %bitcast.72, bf16[512,512]{1,0:T(8,128)(2,1)S(1)} %copy-done.7), kind=kOutput, calls=%fused_computation.46 | convolution fusion | flops 6448742400 | bytes 25690112 | tf_op jit(solution)/shard_map/mi,ikc->mkc/dot_general | solution.py:51
  1240.3 16.7 %copy.67 = bf16[512,32,384]{2,1,0:T(8,128)(2,1)} copy(bf16[512,32,384]{0,2,1:T(8,128)(2,1)} %convert_bitcast_fusion.1) | data formatting | bytes 25165824 | tf_op jit(solution)/shard_map/convert_element_type | solution.py:52
  1257.1 0.0 all-gather.2.cloned.1.call-update
  1257.1 0.0 all-reduce.6.cloned.1.call-start
  1257.2 0.7 slice.128
  1257.9 0.7 slice.133
  1258.6 1.3 collective-permute-start.2
  1259.9 1.3 collective-permute-start.1
  1261.3 37.1 %psum.31 = f32[2,4,384]{2,1,0:T(4,128)S(1)} all-reduce(f32[2,4,384]{2,1,0:T(4,128)S(1)} %pad_maximum_fusion.2), channel_id=1, replica_groups=mesh['grp'=2,'seq'=8,'chan'=2] {'seq'}, use_global_device_ids=true, to_apply=%region_12.0 | all-reduce | flops 3072 | bytes 24576 | tf_op jit(solution)/shard_map/psum | solution.py:103
  1298.4 0.6 broadcast_multiply_fusion.2
  1299.0 12.3 convolution_bitcast_fusion
  1311.3 29.9 %fusion.34 = f32[512,512]{1,0:T(8,128)} fusion(bf16[512,32,384]{2,1,0:T(8,128)(2,1)} %bitcast.73, bf16[512,32,384]{2,1,0:T(8,128)(2,1)} %bitcast.75), kind=kOutput, calls=%fused_computation.55 | convolution fusion | flops 6442450944 | bytes 26214400 | tf_op jit(solution)/shard_map/mkc,ikc->mi/dot_general | solution.py:74
  1341.2 0.0 all-reduce.6.cloned.1.call-update
  1341.2 0.2 all-reduce.4.cloned.1.call-start
  1341.4 0.0 all-gather.2.cloned.1.call-done
  1341.5 21.0 %fusion.46 = f32[768,384]{1,0:T(8,128)} fusion(bf16[16384,768]{1,0:T(8,128)(2,1)} %all-gather.2.cloned.1.call-done, bf16[16384,384]{1,0:T(8,128)(2,1)} %bitcast.67), kind=kOutput, calls=%fused_computation.78 | convolution fusion | flops 9663676416 | bytes 38928384 | tf_op jit(solution)/shard_map/dot_general | solution.py:62
  1362.4 0.0 all-reduce.4.cloned.1.call-update
  1362.4 0.0 copy-start.1
  1362.5 0.0 collective-permute-done.2
  1362.5 0.0 collective-permute-done.1
  1362.5 94.6 %fusion.5 = bf16[16384,384]{1,0:T(8,128)(2,1)} fusion(f32[3,384]{1,0:T(4,128)S(1)} %collective-permute-done.2, f32[3,384]{1,0:T(4,128)S(1)} %collective-permute-done.1, f32[16384,384]{1,0:T(8,128)} %get-tuple-element.28, f32[16384,384]{1,0:T(8,128)} %get-tuple-element.27, bf16[16384,384]{1,0:T(8,128)(2,1)} %param.8, f32[384]{0:T(512)S(1)} %get-tuple-element.23, ...), kind=kLoop, calls=%fused_computation.9 | loop fusion | flops 150994944 | bytes 75518976 | tf_op jit(solution)/shard_map/convert_element_type | solution.py:106
  1457.1 1.7 broadcast_multiply_fusion.1
  1458.7 2.3 broadcast_multiply_fusion
  1461.1 54.8 %all-reduce.4.cloned.1.call-done = f32[768,384]{1,0:T(8,128)} async-done(((f32[768,384]{1,0:T(8,128)}), f32[768,384]{1,0:T(8,128)}) %all-reduce.4.cloned.1.call-update) | async-done | bytes 1179664 | tf_op jit(solution)/shard_map/psum | solution.py:103
  1515.8 2.2 multiply_convert_fusion.2
  1518.0 0.0 copy-done.1
  (15 shorter events, 0.1 us)
Async XLA Ops:
  7.2 301.0 %copy-start = (bf16[768,384]{1,0:T(8,128)(2,1)S(1)}, bf16[768,384]{1,0:T(8,128)(2,1)}, u32[]{:S(2)}) copy-start(bf16[768,384]{1,0:T(8,128)(2,1)} %param.13) | copy-start | bytes 1769476
  7.2 389.1 %reduce-scatter.2.cloned.1.call-start = ((), (), s32[]{:S(2)}) async-start(), calls=%async_computation.4 | async-start | bytes 75497472 | tf_op jit(solution)/shard_map/reduce_scatter | solution.py:71
  333.7 75.8 %copy-start.6 = (bf16[512,512]{1,0:T(8,128)(2,1)S(1)}, bf16[512,512]{1,0:T(8,128)(2,1)}, u32[]{:S(2)}) copy-start(bf16[512,512]{1,0:T(8,128)(2,1)} %param.12) | copy-start | bytes 1572868
  442.9 27.1 %copy-start.5 = (f32[2,4,384]{2,1,0:T(4,128)S(1)}, f32[2,4,384]{2,1,0:T(4,128)}, u32[]{:S(2)}) copy-start(f32[2,4,384]{2,1,0:T(4,128)} %param.9) | copy-start | bytes 36868
  459.7 279.3 %all-to-all-start.1 = ((bf16[512,32,384]{2,1,0:T(8,128)(2,1)}), bf16[512,32,384]{2,1,0:T(8,128)(2,1)}, u32[]{:S(2)}, u32[]{:S(2)}) async-start(bf16[512,32,384]{2,1,0:T(8,128)(2,1)} %copy.59), calls=%async_computation.2 | async-start | bytes 25165824 | tf_op jit(solution)/shard_map/all_to_all | solution.py:80
  465.4 876.0 %all-gather.2.cloned.1.call-start = ((), (), s32[]{:S(2)}) async-start(), calls=%async_computation.5 | async-start | bytes 37748736 | tf_op jit(solution)/shard_map/all_gather | solution.py:63
  466.2 101.2 %collective-permute-start = (bf16[3,384]{1,0:T(4,128)(2,1)S(1)}, bf16[3,384]{1,0:T(4,128)(2,1)S(1)}, u32[]{:S(2)}, u32[]{:S(2)}) collective-permute-start(bf16[3,384]{1,0:T(4,128)(2,1)S(1)} %slice.105), channel_id=1, source_target_pairs={{0,2},{2,4},{4,6},{6,8},{8,10},{10,12},{12,14},{1,3},{3,5},{5,7},{... | collective-permute-start | bytes 6920 | tf_op jit(solution)/shard_map/ppermute | solution.py:10
  746.5 9.6 copy-start.3
  756.1 10.0 copy-start.4
  766.1 12.0 copy-start.2
  908.3 299.8 %copy-start.7 = (bf16[512,512]{1,0:T(8,128)(2,1)S(1)}, bf16[512,512]{1,0:T(8,128)(2,1)}, u32[]{:S(2)}) copy-start(bf16[512,512]{1,0:T(8,128)(2,1)} %param.12) | copy-start | bytes 1572868
  1257.1 200.0 %all-reduce.6.cloned.1.call-start = ((), (), s32[]{:S(2)}) async-start(), calls=%async_computation.7 | async-start | bytes 2621440 | tf_op jit(solution)/shard_map/psum | solution.py:104
  1258.6 103.8 %collective-permute-start.2 = (f32[3,384]{1,0:T(4,128)S(1)}, f32[3,384]{1,0:T(4,128)S(1)}, u32[]{:S(2)}, u32[]{:S(2)}) collective-permute-start(f32[3,384]{1,0:T(4,128)S(1)} %slice.133), channel_id=1, source_target_pairs={{2,0},{4,2},{6,4},{8,6},{10,8},{12,10},{14,12},{3,1},{5,3},{7,5},{... | collective-permute-start | bytes 13832 | tf_op jit(solution)/shard_map/ppermute | solution.py:10
  1259.9 102.6 %collective-permute-start.1 = (f32[3,384]{1,0:T(4,128)S(1)}, f32[3,384]{1,0:T(4,128)S(1)}, u32[]{:S(2)}, u32[]{:S(2)}) collective-permute-start(f32[3,384]{1,0:T(4,128)S(1)} %slice.128), channel_id=1, source_target_pairs={{2,0},{4,2},{6,4},{8,6},{10,8},{12,10},{14,12},{3,1},{5,3},{7,5},{... | collective-permute-start | bytes 13832 | tf_op jit(solution)/shard_map/ppermute | solution.py:10
  1341.2 174.6 %all-reduce.4.cloned.1.call-start = ((), (), s32[]{:S(2)}) async-start(), calls=%async_computation.6 | async-start | bytes 2359296 | tf_op jit(solution)/shard_map/psum | solution.py:103
  1362.4 155.6 %copy-start.1 = (bf16[768,384]{1,0:T(8,128)(2,1)S(1)}, bf16[768,384]{1,0:T(8,128)(2,1)}, u32[]{:S(2)}) copy-start(bf16[768,384]{1,0:T(8,128)(2,1)} %param.13) | copy-start | bytes 1769476
Sparse Core Ops, SparseCore 0:
  333.8 62.3 reduce-scatter.1
  1257.2 41.0 all-gather.1
  1341.3 91.1 all-reduce.5
  1435.9 79.9 all-reduce.3
where the time goes:
time: 1530 us; the launch traced here: 1520 us
  blocking collectives  607 us (40%)
  waiting for transfers between devices  372 us (24%)
  other arithmetic  247 us (16%)
  matrix products  177 us (12%)
  local copies, waits for them, and re-layouts  93.9 us (6%)
    all_to_all x1, blocking collectives, body(): lax.all_to_all(twisted, 'seq', split_axis=1, concat_axis=0, tiled=True)  290 us
    all_to_all x1, blocking collectives, body(): lax.all_to_all(cotangent.reshape(blocks, inner_size, channels), 'seq', sp...  280 us
    all_to_all x1, waiting for transfers between devices, body(): lax.all_to_all(twisted_grad_turned, 'seq', split_axis=0, concat_axis=1, t...  157 us
    ppermute x3, waiting for transfers between devices, passed_along(): return lax.ppermute(array, axis, pairs)  97.2 us
    convert_element_type x1, other arithmetic, body(): input_grad.astype(jnp.bfloat16)  94.6 us
    reduce_sum x1, other arithmetic, taps_grad(): jnp.sum(signal * history_rows[3 - offset:3 - offset + tokens], 0)  79.5 us
    reduce_scatter x1, waiting for transfers between devices, body(): lax.psum_scatter(full_terms, 'chan', scatter_dimension=1, tiled=True)  62.5 us
    psum x1, waiting for transfers between devices, body(): proj_sum, conv_sum = lax.psum((proj_part, conv_part), 'seq')  54.8 us
  transfers between devices with their start and end apart: 8, of which 4 were waited for; matrix products, arithmetic and copies ran while one was open for 12% of the time, Pallas kernels for 0%

commit v1 on v0

v1 whole, which is shorter than its diff:
```python
import functools

import jax
import jax.numpy as jnp
from jax import lax
from jax.experimental import pallas as pl
from jax.experimental.pallas import tpu as pltpu
from jax.sharding import PartitionSpec as P

CHUNKS = 3


def passed_along(array, axis, by):
    peers = lax.axis_size(axis)
    pairs = [(i, i + by) for i in range(peers) if 0 <= i + by < peers]
    return lax.ppermute(array, axis, pairs)


def causal_taps(history_rows, weights, tokens):
    result = weights[0] * history_rows[3 : 3 + tokens]
    for offset in range(1, 4):
        result = result + weights[offset] * history_rows[3 - offset : 3 - offset + tokens]
    return result


def exchange(blocks):
    peers = len(blocks)
    received = [blocks[0]]
    for step in range(1, peers):
        pairs = [(i, (i + step) % peers) for i in range(peers)]
        received.append(lax.ppermute(blocks[step], "seq", pairs))
    return received


def by_source(array, axis, peers, me):
    shape = array.shape
    size = shape[axis] // peers
    parts = [lax.slice_in_dim(array, b * size, (b + 1) * size, axis=axis) for b in range(peers)]
    backwards = jnp.concatenate(parts[::-1] * 2, axis)
    return lax.dynamic_slice_in_dim(backwards, (peers - 1 - me) * size, shape[axis], axis)


def by_target(array, axis, peers, me):
    size = array.shape[axis] // peers
    twice = jnp.concatenate([array, array], axis)
    return lax.dynamic_slice_in_dim(twice, me * size, array.shape[axis], axis)


def tail_kernel(
    parts, *refs
):
    grad_refs = refs[:parts]
    (inputs_ref, before_ref, last_ref, cot_ref, weight_ref, mix_ref, halo_ref) = refs[parts : parts + 7]
    (out_ref, inner_ref, conv_ref) = refs[-6:-3]
    (signal, value_ext, gate_ext) = refs[-3:]
    step = pl.program_id(0)
    steps = pl.num_programs(0)
    rows = inputs_ref.shape[0]
    taps = weight_ref.shape[1]

    @pl.when(step == 0)
    def _():
        inner_ref[...] = jnp.zeros_like(inner_ref)
        conv_ref[...] = jnp.zeros_like(conv_ref)
        value_ext[0:8] = halo_ref[0]
        gate_ext[0:8] = halo_ref[1]

    value_ext[rows : rows + 8] = value_ext[0:8]
    gate_ext[rows : rows + 8] = gate_ext[0:8]
    signal[8 : 8 + rows] = inputs_ref[...].astype(jnp.float32)
    before = before_ref[...].astype(jnp.float32)[8:16]
    signal[0:8] = jnp.where(step == steps - 1, last_ref[...], before)
    weight = weight_ref[...]
    shifted = [signal[8 - s : 8 - s + rows] for s in range(taps)]
    value_conv = weight[0, 0][None] * shifted[0]
    gate_conv = weight[1, 0][None] * shifted[0]
    for s in range(1, taps):
        value_conv = value_conv + weight[0, s][None] * shifted[s]
        gate_conv = gate_conv + weight[1, s][None] * shifted[s]
    gate_sig = jax.nn.sigmoid(gate_conv)
    value_part = value_conv * gate_sig
    gated = value_part.astype(jnp.bfloat16)
    if parts > 1:
        grad = jnp.concatenate([ref[0] for ref in grad_refs], 0)
    else:
        grad = grad_refs[0][0]
    inner_ref[...] += lax.dot_general(
        grad, gated, (((1,), (1,)), ((), ())), preferred_element_type=jnp.float32
    )
    gated_grad = jnp.dot(mix_ref[...], grad, preferred_element_type=jnp.float32)
    value_grad = gated_grad * gate_sig
    gate_grad = gated_grad * value_part * (1.0 - gate_sig)
    value_ext[0:rows] = value_grad
    gate_ext[0:rows] = gate_grad
    for s in range(taps):
        conv_ref[0, s] += jnp.sum((value_grad * shifted[s]).reshape(rows // 8, 8, -1), 0)
        conv_ref[1, s] += jnp.sum((gate_grad * shifted[s]).reshape(rows // 8, 8, -1), 0)
    total = cot_ref[...].astype(jnp.float32)
    for s in range(taps):
        total = total + weight[0, s][None] * value_ext[s : s + rows]
        total = total + weight[1, s][None] * gate_ext[s : s + rows]
    out_ref[...] = total.astype(jnp.bfloat16)


def tail(grads, inputs, last_rows, cotangent, conv_weight, mix_turned, halo, chunk, width, result):
    tokens, channels = inputs.shape
    inner_size = mix_turned.shape[0]
    blocks = tokens // inner_size
    parts = len(grads)

    def place(step):
        return blocks - 1 - step

    ratio = inner_size // 16
    in_specs = [
        pl.BlockSpec((1, g.shape[1], width), lambda step: (place(step), 0, 0)) for g in grads
    ] + [
        pl.BlockSpec((inner_size, width), lambda step: (place(step), chunk)),
        pl.BlockSpec((16, width), lambda step: (jnp.maximum(place(step) * ratio - 1, 0), chunk)),
        pl.BlockSpec((8, width), lambda step: (0, chunk)),
        pl.BlockSpec((inner_size, width), lambda step: (place(step), chunk)),
        pl.BlockSpec((2, 4, width), lambda step: (0, 0, chunk)),
        pl.BlockSpec((inner_size, inner_size), lambda step: (0, 0)),
        pl.BlockSpec((2, 8, width), lambda step: (0, 0, 0)),
    ]
    operands = [*grads, inputs, inputs, last_rows, cotangent, conv_weight, mix_turned, halo]
    aliases = {}
    if result is not None:
        aliases = {len(operands): 0}
        operands.append(result)
        in_specs.append(pl.BlockSpec(memory_space=pl.ANY))
    return pl.pallas_call(
        functools.partial(tail_kernel, parts),
        grid=(blocks,),
        in_specs=in_specs,
        out_specs=[
            pl.BlockSpec((inner_size, width), lambda step: (place(step), chunk)),
            pl.BlockSpec((inner_size, inner_size), lambda step: (0, 0)),
            pl.BlockSpec((2, 4, 8, width), lambda step: (0, 0, 0, 0)),
        ],
        out_shape=[
            jax.ShapeDtypeStruct((tokens, channels), jnp.bfloat16),
            jax.ShapeDtypeStruct((inner_size, inner_size), jnp.float32),
            jax.ShapeDtypeStruct((2, 4, 8, width), jnp.float32),
        ],
        scratch_shapes=[pltpu.VMEM((inner_size + 8, width), jnp.float32)] * 3,
        input_output_aliases=aliases,
        compiler_params=pltpu.CompilerParams(vmem_limit_bytes=32 * 1024 * 1024),
        cost_estimate=pl.CostEstimate(
            flops=tokens * width * inner_size * 16,
            bytes_accessed=tokens * width * 8,
            transcendentals=tokens * width,
        ),
    )(*operands)


def body(inputs, cotangent, conv_weight, mix_inner, twiddle, mix_outer, proj_weight):
    peers = lax.axis_size("seq")
    me = lax.axis_index("seq")
    half = lax.axis_index("chan")
    halves = lax.axis_size("chan")
    inner_size = mix_inner.shape[0]
    outer_size = mix_outer.shape[0]
    tokens, channels = inputs.shape
    blocks = tokens // inner_size
    cols = inner_size // peers
    grad_scale = (outer_size * inner_size) ** (-0.5)

    cot_blocks = cotangent.reshape(blocks, inner_size, channels)
    cot_sends = [
        lax.dynamic_slice_in_dim(cot_blocks, lax.rem(me + s, peers) * cols, cols, 1)
        for s in range(peers)
    ]
    cot_parts = exchange(cot_sends)
    last_rows = passed_along(inputs[tokens - 3 :], "seq", 1)
    twiddle_all = lax.all_gather(twiddle, "seq", axis=0, tiled=True)
    swap = [(i, halves - 1 - i) for i in range(halves)]
    weight_all = lax.all_gather(proj_weight, "chan", axis=1, tiled=True)
    weight_rows = lax.dynamic_slice_in_dim(weight_all, half * channels, channels, 0)

    history_rows = jnp.concatenate([last_rows, inputs], 0).astype(jnp.float32)
    value_conv = causal_taps(history_rows, conv_weight[0], tokens)
    gate_conv = causal_taps(history_rows, conv_weight[1], tokens)
    gated_input = (value_conv * jax.nn.sigmoid(gate_conv)).astype(jnp.bfloat16)
    gated_blocks = gated_input.reshape(blocks, inner_size, channels)
    mix_target = by_target(mix_inner, 0, peers, me)
    twiddle_target = by_target(twiddle, 1, peers, me)
    inner_mixed = jnp.einsum(
        "kj,ijc->ikc", mix_target, gated_blocks, preferred_element_type=jnp.float32
    )
    twisted = (inner_mixed * twiddle_target[:, :, None]).astype(jnp.bfloat16)
    twisted, cot_parts = lax.optimization_barrier((twisted, cot_parts))
    twisted_parts = exchange([twisted[:, s * cols : (s + 1) * cols] for s in range(peers)])

    cot_turned = jnp.concatenate(cot_parts, 0)
    cot_wide = lax.all_gather(cot_turned, "chan", axis=2, tiled=True)
    outer_rows = by_source(mix_outer, 0, peers, me)
    outer_target = by_target(outer_rows, 1, peers, me)
    twiddle_cols = lax.dynamic_slice_in_dim(twiddle_all, me * cols, cols, 1)
    twiddle_cols = by_target(twiddle_cols, 0, peers, me)
    mixed_grad = jnp.einsum(
        "mkd,cd->mkc", cot_wide, weight_rows, preferred_element_type=jnp.float32
    ).astype(jnp.bfloat16)
    width = channels // CHUNKS
    grad_parts = []
    for chunk in range(CHUNKS):
        piece = mixed_grad[:, :, chunk * width : (chunk + 1) * width]
        twisted_grad = jnp.einsum(
            "mi,mkc->ikc", outer_target, piece, preferred_element_type=jnp.float32
        ).astype(jnp.bfloat16)
        turned = (twisted_grad.astype(jnp.float32) * twiddle_cols[:, :, None]).astype(jnp.bfloat16)
        grad_parts.append(exchange([turned[s * blocks : (s + 1) * blocks] for s in range(peers)]))

    received = jnp.concatenate(twisted_parts, 0)
    outer_both = by_source(outer_rows, 1, peers, me)
    mixed = jnp.einsum(
        "mi,ikc->mkc", outer_both, received, preferred_element_type=jnp.float32
    ).astype(jnp.bfloat16)
    outer_part = jnp.einsum(
        "mkc,ikc->mi", mixed_grad, received, preferred_element_type=jnp.float32
    )
    outer_part = by_source(by_source(outer_part, 0, peers, me), 1, peers, me)
    proj_part = lax.dot_general(
        mixed.reshape(-1, channels),
        cot_wide.reshape(-1, channels * halves),
        (((0,), (0,)), ((), ())),
        preferred_element_type=jnp.float32,
    )
    own = lax.dynamic_slice_in_dim(proj_part, half * channels, channels, 1)
    other = lax.dynamic_slice_in_dim(proj_part, (halves - 1 - half) * channels, channels, 1)
    other = lax.ppermute(other, "chan", swap)
    proj_part = jnp.where(
        half == 0, jnp.concatenate([own, other], 0), jnp.concatenate([other, own], 0)
    )
    proj_sum = lax.psum(proj_part, "seq")
    outer_sum = lax.psum(outer_part, ("seq", "chan"))

    mix_source = by_source(mix_inner, 0, peers, me)
    mix_turned = mix_source.T
    pad_rows = jnp.concatenate([jnp.zeros((5, channels), jnp.bfloat16), last_rows], 0)
    pad_rows = pad_rows.astype(jnp.float32)
    first_history = jnp.concatenate([last_rows, inputs[:3]], 0).astype(jnp.float32)
    first_value = causal_taps(first_history, conv_weight[0], 3)
    first_sig = jax.nn.sigmoid(causal_taps(first_history, conv_weight[1], 3))
    result = None
    inner_part = 0.0
    conv_parts = []
    for chunk in range(CHUNKS):
        grads = grad_parts[chunk]
        lanes = slice(chunk * width, (chunk + 1) * width)
        first = jnp.concatenate([g[0] for g in grads], 0)
        first_grad = lax.dot_general(
            mix_source[:, :3], first, (((0,), (0,)), ((), ())), preferred_element_type=jnp.float32
        )
        sig = first_sig[:, lanes]
        edge = jnp.stack([first_grad * sig, first_grad * first_value[:, lanes] * sig * (1.0 - sig)])
        halo = passed_along(edge, "seq", -1)
        halo = jnp.concatenate([halo, jnp.zeros((2, 5, width), jnp.float32)], 1)
        if cols % 16:
            grads = [jnp.concatenate(grads, 1)]
        result, inner_one, conv_one = tail(
            grads, inputs, pad_rows, cotangent, conv_weight, mix_turned, halo, chunk, width, result
        )
        inner_part = inner_part + inner_one
        conv_parts.append(jnp.sum(conv_one, 2))
    inner_part = by_source(inner_part, 0, peers, me)
    conv_sum = lax.psum(jnp.concatenate(conv_parts, 2), "seq")
    inner_sum = lax.psum(inner_part, ("seq", "chan"))
    return (
        result,
        (proj_sum * grad_scale).astype(jnp.bfloat16),
        inner_sum * grad_scale,
        outer_sum * grad_scale,
        conv_sum * grad_scale,
    )


def solution(mesh):
    in_specs = (
        P(("grp", "seq"), "chan"),
        P(("grp", "seq"), "chan"),
        P(None, None, "chan"),
        P(),
        P("seq", None),
        P(),
        P(None, "chan"),
    )
    out_specs = (
        P(("grp", "seq"), "chan"),
        P("grp", "chan"),
        P("grp", None),
        P("grp", None),
        P("grp", None, "chan"),
    )
    return jax.shard_map(body, mesh=mesh, in_specs=in_specs, out_specs=out_specs, check_vma=False)
```

time: 1530 us -> 1630 us (1.065)
  blocking collectives: 607 us -> 140 us
  starting transfers between devices: 12.5 us -> 478 us
  local copies, waits for them, and re-layouts: 93.9 us -> 307 us
  other arithmetic: 247 us -> 90.7 us
  Pallas kernels: 0 us -> 129 us
  matrix products: 177 us -> 87.5 us
    all_to_all x2 -> x0, blocking collectives: 570 us -> none  [the longest x1 290 us: body(): lax.all_to_all(twisted, 'seq', split_axis=1, concat_axis=0, tiled=True)]
    ppermute x0 -> x36, starting transfers between devices: none -> 471 us  [the longest x35 471 us: exchange(): received.append(lax.ppermute(blocks[step], 'seq', pairs))]
    ppermute x0 -> x36, waiting for transfers between devices: none -> 218 us  [the longest x35 218 us: exchange(): received.append(lax.ppermute(blocks[step], 'seq', pairs))]
    all_to_all x1 -> x0, waiting for transfers between devices: 157 us -> none  [body(): lax.all_to_all(twisted_grad_turned, 'seq', split_axis=0, concat_axis=1, t...]
    pallas_call x0 -> x3, Pallas kernels: none -> 129 us  [tail(): pl.pallas_call(functools.partial(tail_kernel, parts), grid=(blocks,), in_...]
    slice x4 -> x16, local copies, waits for them, and re-layouts: 2.16 us -> 97.1 us  [the longest x8 87.8 us: body(): twisted[:, s * cols:(s + 1) * cols]]
    dot_general x8 -> x10, matrix products: 177 us -> 87.5 us  [the longest x1 25.9 us: body(): lax.dot_general(mixed.reshape(-1, channels), cot_wide.reshape(-1, channel...]
    unnamed x16 -> x169, local copies, waits for them, and re-layouts: 1.45 us -> 90.5 us
  transfers between devices with their start and end apart: 8 -> 44, of which waited for: 4 -> 17; matrix products, arithmetic and copies ran while one was open for 12% -> 24% of each run, Pallas kernels for 0% -> 8%
where the time goes in v1:
time: 1630 us; the launch traced here: 1610 us
  starting transfers between devices  478 us (29%)
  waiting for transfers between devices  366 us (22%)
  local copies, waits for them, and re-layouts  307 us (19%)
  blocking collectives  140 us (9%)
  Pallas kernels  129 us (8%)
  other arithmetic  90.7 us (6%)
  matrix products  87.5 us (5%)
    ppermute x35, starting transfers between devices, exchange(): received.append(lax.ppermute(blocks[step], 'seq', pairs))  471 us
    ppermute x35, waiting for transfers between devices, exchange(): received.append(lax.ppermute(blocks[step], 'seq', pairs))  218 us
    pallas_call x3, Pallas kernels, tail(): pl.pallas_call(functools.partial(tail_kernel, parts), grid=(blocks,), in_...  129 us
    unnamed x169, local copies, waits for them, and re-layouts  90.5 us
    slice x8, local copies, waits for them, and re-layouts, body(): twisted[:, s * cols:(s + 1) * cols]  87.8 us
    all_gather x1, blocking collectives, body(): twiddle_all = lax.all_gather(twiddle, 'seq', axis=0, tiled=True)  82.6 us
    psum x1, waiting for transfers between devices, body(): proj_sum = lax.psum(proj_part, 'seq')  79.3 us
    psum x1, blocking collectives, body(): conv_sum = lax.psum(jnp.concatenate(conv_parts, 2), 'seq')  57.1 us
  transfers between devices with their start and end apart: 44, of which 17 were waited for; matrix products, arithmetic and copies ran while one was open for 24% of the time, Pallas kernels for 8%

profile of v1, /device:TPU:0, one launch (start us, length us, event | category | flops | bytes accessed | tf_op | source)
XLA Modules:
  0.0 1612.5 jit_solution(14502114859907258487)
XLA Ops:
  7.3 7.3 constant_dynamic-slice_fusion.7
  44.0 9.3 collective-permute-done
  53.3 37.6 %collective-permute-start.5 = (bf16[64,32,384]{2,0,1:T(8,128)(2,1)}, bf16[64,32,384]{2,0,1:T(8,128)(2,1)S(1)}, u32[]{:S(2)}, u32[]{:S(2)}) collective-permute-start(bf16[64,32,384]{2,0,1:T(8,128)(2,1)} %copy.215), channel_id=1, source_target_pairs={{0,10},{2,12},{4,14},{6,0},{8,2},{10,4},{12,6},{14,8},{1,11},{3,13... | collective-permute-start | bytes 4718600 | tf_op jit(solution)/shard_map/ppermute | solution.py:31
  90.9 14.2 maximum_convert_fusion
  105.2 39.1 %multiply_convert_fusion.1 = bf16[16384,384]{1,0:T(8,128)(2,1)} fusion(f32[16387,384]{1,0:T(8,128)} %maximum_convert_fusion, f32[384]{0:T(512)S(1)} %get-tuple-element.42, f32[384]{0:T(512)S(1)} %get-tuple-element.43, f32[384]{0:T(512)S(1)} %get-tuple-element.44, f32[384]{0:T(512)S(1)} %get-tuple-element.45, f32[384]{0:T(512)S(1)} %get-tuple-element.46, ...), kind=kLoop, calls=%fused_computation.1 | loop fusion | flops 119537664 | bytes 113258496 | tf_op jit(solution)/shard_map/convert_element_type | solution.py:184
  144.4 169.5 %collective-permute-start.6 = (bf16[64,32,384]{2,0,1:T(8,128)(2,1)}, bf16[64,32,384]{2,0,1:T(8,128)(2,1)}, u32[]{:S(2)}, u32[]{:S(2)}) collective-permute-start(bf16[64,32,384]{2,0,1:T(8,128)(2,1)} %copy.216), channel_id=1, source_target_pairs={{0,12},{2,14},{4,0},{6,2},{8,4},{10,6},{12,8},{14,10},{1,13},{3,15... | collective-permute-start | bytes 4718600 | tf_op jit(solution)/shard_map/ppermute | solution.py:31
  316.3 12.8 fusion
  329.0 20.0 %collective-permute-done.6 = bf16[64,32,384]{2,0,1:T(8,128)(2,1)} collective-permute-done((bf16[64,32,384]{2,0,1:T(8,128)(2,1)}, bf16[64,32,384]{2,0,1:T(8,128)(2,1)}, u32[]{:S(2)}, u32[]{:S(2)}) %collective-permute-start.6) | collective-permute-done | bytes 1572896 | tf_op jit(solution)/shard_map/ppermute | solution.py:31
  349.0 31.3 %collective-permute-done.7 = bf16[64,32,384]{2,0,1:T(8,128)(2,1)} collective-permute-done((bf16[64,32,384]{2,0,1:T(8,128)(2,1)}, bf16[64,32,384]{2,0,1:T(8,128)(2,1)}, u32[]{:S(2)}, u32[]{:S(2)}) %collective-permute-start.7) | collective-permute-done | bytes 1572896 | tf_op jit(solution)/shard_map/ppermute | solution.py:31
  400.3 43.1 %fusion.44 = (bf16[64,32,384]{1,2,0:T(8,128)(2,1)}, bf16[64,32,384]{1,2,0:T(8,128)(2,1)}, bf16[64,32,384]{1,2,0:T(8,128)(2,1)}, bf16[64,32,384]{1,2,0:T(8,128)(2...) fusion(bf16[64,256,384]{1,2,0:T(8,128)(2,1)} %fusion), kind=kLoop, calls=%fused_computation.213 | loop fusion | bytes 62914560 | tf_op jit(solution)/shard_map/slice | solution.py:193
  443.4 6.4 copy.180
  449.8 6.4 copy.181
  456.2 15.9 collective-permute-start.33
  472.1 82.6 %all_gather.11 = f32[512,256]{1,0:T(8,128)S(1)} all-gather(f32[64,256]{1,0:T(8,128)S(1)} %copy-done.13), channel_id=1, replica_groups=mesh['grp'=2,'seq'=8,'chan'=2] {'seq'}, dimensions={0}, use_global_device_ids=true | all-gather | bytes 589824 | tf_op jit(solution)/shard_map/all_gather | solution.py:176
  574.0 6.4 copy.182
  580.6 6.4 copy.183
  587.3 6.4 copy.184
  593.7 3.8 collective-permute-start.36
  597.5 6.4 copy.185
  603.9 6.4 copy.186
  619.0 4.6 copy.187
  623.6 6.3 copy.188
  630.0 49.1 %collective-permute-done.34 = bf16[64,32,384]{2,1,0:T(8,128)(2,1)} collective-permute-done((bf16[64,32,384]{2,1,0:T(8,128)(2,1)}, bf16[64,32,384]{2,1,0:T(8,128)(2,1)}, u32[]{:S(2)}, u32[]{:S(2)}) %collective-permute-start.34) | collective-permute-done | bytes 1572896 | tf_op jit(solution)/shard_map/ppermute | solution.py:31
  679.0 6.3 copy.189
  685.3 25.9 %collective-permute-done.35 = bf16[64,32,384]{2,1,0:T(8,128)(2,1)} collective-permute-done((bf16[64,32,384]{2,1,0:T(8,128)(2,1)}, bf16[64,32,384]{2,1,0:T(8,128)(2,1)}, u32[]{:S(2)}, u32[]{:S(2)}) %collective-permute-start.35) | collective-permute-done | bytes 1572896 | tf_op jit(solution)/shard_map/ppermute | solution.py:31
  711.2 6.3 copy.190
  717.5 6.3 copy.191
  723.8 6.3 copy.192
  730.1 12.7 collective-permute-done.38
  742.8 6.3 copy.193
  749.1 6.4 constant_dynamic-update-slice_fusion.54
  755.5 6.3 constant_dynamic-update-slice_fusion.53
  764.9 3.5 constant_dynamic-update-slice_fusion.51
  768.4 6.4 constant_dynamic-update-slice_fusion.50
  780.9 45.9 %copy.195 = bf16[512,32,384]{2,0,1:T(8,128)(2,1)} copy(bf16[512,32,384]{1,2,0:T(8,128)(2,1)} %constant_dynamic-update-slice_fusion.48) | data formatting | bytes 25165824 | tf_op jit(solution)/shard_map/concatenate | solution.py:214
  826.8 21.5 %convolution_convert_fusion = bf16[512,32,384]{2,0,1:T(8,128)(2,1)} fusion(bf16[512,32,768]{2,0,1:T(8,128)(2,1)} %all-gather.3.cloned.1.call-done, bf16[768,768]{1,0:T(8,128)(2,1)} %all-gather.5.cloned.1.call-done, s32[]{:T(128)S(6)} %select_n.71), kind=kOutput, calls=%fused_computation.13 | convolution fusion | flops 9669967872 | bytes 38338564 | tf_op jit(solution)/shard_map/mkd,cd->mkc/dot_general | solution.py:201
  848.3 4.7 fusion.7
  856.5 4.3 fusion.5
  860.8 13.4 convolution_bitcast_fusion
  877.1 26.3 %multiply_convert_fusion.2 = (bf16[512,32,128]{2,1,0:T(8,128)(2,1)S(1)}, bf16[512,32,128]{2,1,0:T(8,128)(2,1)S(1)}, bf16[512,32,128]{2,1,0:T(8,128)(2,1)S(1)}) fusion(bf16[512,32,128]{2,0,1:T(8,128)(2,1)S(1)} %copy-done.6, f32[512,32]{1,0:T(8,128)S(1)} %copy-done.8, bf16[512,32,128]{2,0,1:T(8,128)(2,1)S(1)} %fusion.7, bf16[512,32,128]{2,0,1:T(8,128)(2,1)S(1)} %fusion.9), kind=kLoop, calls=%fused_computation.9 | loop fusion | flops 18874368 | bytes 25231360 | tf_op jit(solution)/shard_map/convert_element_type | solution.py:211
  905.9 16.1 %collective-permute-start.24 = (bf16[64,32,128]{2,1,0:T(8,128)(2,1)}, bf16[64,32,128]{2,1,0:T(8,128)(2,1)S(1)}, u32[]{:S(2)}, u32[]{:S(2)}) collective-permute-start(bf16[64,32,128]{2,1,0:T(8,128)(2,1)} %get-tuple-element.75), channel_id=1, source_target_pairs={{0,2},{2,4},{4,6},{6,8},{8,10},{10,12},{12,14},{14,0},{1,3},{3,5},... | collective-permute-start | bytes 1572872 | tf_op jit(solution)/shard_map/ppermute | solution.py:31
  922.0 63.9 %collective-permute-start.25 = (bf16[64,32,128]{2,1,0:T(8,128)(2,1)}, bf16[64,32,128]{2,1,0:T(8,128)(2,1)S(1)}, u32[]{:S(2)}, u32[]{:S(2)}) collective-permute-start(bf16[64,32,128]{2,1,0:T(8,128)(2,1)} %get-tuple-element.74), channel_id=1, source_target_pairs={{0,4},{2,6},{4,8},{6,10},{8,12},{10,14},{12,0},{14,2},{1,5},{3,7},... | collective-permute-start | bytes 1572872 | tf_op jit(solution)/shard_map/ppermute | solution.py:31
  985.9 5.3 collective-permute-start.27
  998.6 4.9 concatenate.94
  1003.5 25.9 %fusion.11 = f32[384,768]{1,0:T(8,128)} fusion(bf16[512,32,768]{2,0,1:T(8,128)(2,1)} %all-gather.3.cloned.1.call-done, bf16[512,32,384]{2,0,1:T(8,128)(2,1)} %copy.195, bf16[512,1024]{0,1:T(8,128)(2,1)} %constant_dynamic-update-slice_fusion.32, s32[]{:T(128)S(6)} %select_n.60), kind=kOutput, calls=%fused_computation.21 | convolution fusion | flops 16112418816 | bytes 39452676 | tf_op jit(solution)/shard_map/dot_general | solution.py:223
  1034.6 5.0 collective-permute-done.26.refs_3_
  1040.0 26.1 %collective-permute-start.9 = (bf16[64,32,128]{2,1,0:T(8,128)(2,1)}, bf16[64,32,128]{2,1,0:T(8,128)(2,1)S(1)}, u32[]{:S(2)}, u32[]{:S(2)}) collective-permute-start(bf16[64,32,128]{2,1,0:T(8,128)(2,1)} %get-tuple-element.90), channel_id=1, source_target_pairs={{0,4},{2,6},{4,8},{6,10},{8,12},{10,14},{12,0},{14,2},{1,5},{3,7},... | collective-permute-start | bytes 1572872 | tf_op jit(solution)/shard_map/ppermute | solution.py:31
  1069.5 10.3 collective-permute-start.11
  1079.8 29.3 %collective-permute-start.12 = (bf16[64,32,128]{2,1,0:T(8,128)(2,1)}, bf16[64,32,128]{2,1,0:T(8,128)(2,1)S(1)}, u32[]{:S(2)}, u32[]{:S(2)}) collective-permute-start(bf16[64,32,128]{2,1,0:T(8,128)(2,1)} %get-tuple-element.87), channel_id=1, source_target_pairs={{0,10},{2,12},{4,14},{6,0},{8,2},{10,4},{12,6},{14,8},{1,11},{3,13... | collective-permute-start | bytes 1572872 | tf_op jit(solution)/shard_map/ppermute | solution.py:31
  1112.4 19.6 %collective-permute-done.10.refs_3_ = bf16[64,32,128]{2,1,0:T(8,128)(2,1)S(1)} collective-permute-done((bf16[64,32,128]{2,1,0:T(8,128)(2,1)}, bf16[64,32,128]{2,1,0:T(8,128)(2,1)S(1)}, u32[]{:S(2)}, u32[]{:S(2)}) %collective-permute-start.10) | collective-permute-done | bytes 524320 | tf_op jit(solution)/shard_map/ppermute | solution.py:31
  1132.0 11.7 collective-permute-start.16
  1143.7 19.4 %collective-permute-start.17 = (bf16[64,32,128]{2,1,0:T(8,128)(2,1)}, bf16[64,32,128]{2,1,0:T(8,128)(2,1)S(1)}, u32[]{:S(2)}, u32[]{:S(2)}) collective-permute-start(bf16[64,32,128]{2,1,0:T(8,128)(2,1)} %get-tuple-element.82), channel_id=1, source_target_pairs={{0,4},{2,6},{4,8},{6,10},{8,12},{10,14},{12,0},{14,2},{1,5},{3,7},... | collective-permute-start | bytes 1572872 | tf_op jit(solution)/shard_map/ppermute | solution.py:31
  1163.2 36.7 %collective-permute-start.18 = (bf16[64,32,128]{2,1,0:T(8,128)(2,1)}, bf16[64,32,128]{2,1,0:T(8,128)(2,1)S(1)}, u32[]{:S(2)}, u32[]{:S(2)}) collective-permute-start(bf16[64,32,128]{2,1,0:T(8,128)(2,1)} %get-tuple-element.81), channel_id=1, source_target_pairs={{0,6},{2,8},{4,10},{6,12},{8,14},{10,0},{12,2},{14,4},{1,7},{3,9},... | collective-permute-start | bytes 1572872 | tf_op jit(solution)/shard_map/ppermute | solution.py:31
  1202.4 20.8 %collective-permute-done.18.refs_3_ = bf16[64,32,128]{2,1,0:T(8,128)(2,1)S(1)} collective-permute-done((bf16[64,32,128]{2,1,0:T(8,128)(2,1)}, bf16[64,32,128]{2,1,0:T(8,128)(2,1)S(1)}, u32[]{:S(2)}, u32[]{:S(2)}) %collective-permute-start.18) | collective-permute-done | bytes 524320 | tf_op jit(solution)/shard_map/ppermute | solution.py:31
  1223.2 13.1 collective-permute-done.19.refs_4_
  1236.3 9.9 collective-permute-done.21.refs_6_
  1246.2 10.3 collective-permute-done.22.refs_7_
  1268.7 4.6 copy-done
  1273.2 43.4 %shard_map.110 = (bf16[16384,384]{1,0:T(8,128)(2,1)}, f32[256,256]{1,0:T(8,128)S(1)}, f32[2,4,8,128]{3,2,1,0:T(8,128)S(1)}) custom-call(bf16[64,32,128]{2,1,0:T(8,128)(2,1)S(1)} %get-tuple-element.76.refs_0_, bf16[64,32,128]{2,1,0:T(8,128)(2,1)S(1)} %collective-permute-done.24.refs_1_, bf16[64,32,128]{2,1,0:T(8,128)(2,1)S(1)} %collective-permute-done.25.refs_2_, ...), custom_call_target="tpu_custom_call" | custom-call | flops 8589934592 | bytes 16777216 | tf_op jit(solution)/shard_map/pallas_call | solution.py:132
  1316.6 42.9 %shard_map.111 = (bf16[16384,384]{1,0:T(8,128)(2,1)}, f32[256,256]{1,0:T(8,128)S(1)}, f32[2,4,8,128]{3,2,1,0:T(8,128)S(1)}) custom-call(bf16[64,32,128]{2,1,0:T(8,128)(2,1)S(1)} %get-tuple-element.84.refs_0_, bf16[64,32,128]{2,1,0:T(8,128)(2,1)S(1)} %collective-permute-done.16.refs_1_, ...), custom_call_target="tpu_custom_call", output_to_operand_aliasing={{0}: (15, {})} | custom-call | flops 8589934592 | bytes 16777216 | tf_op jit(solution)/shard_map/pallas_call | solution.py:132
  1359.6 43.0 %shard_map.112 = (bf16[16384,384]{1,0:T(8,128)(2,1)}, f32[256,256]{1,0:T(8,128)S(1)}, f32[2,4,8,128]{3,2,1,0:T(8,128)S(1)}) custom-call(bf16[64,32,128]{2,1,0:T(8,128)(2,1)S(1)} %get-tuple-element.92.refs_0_, bf16[64,32,128]{2,1,0:T(8,128)(2,1)S(1)} %collective-permute-done.8.refs_1_, ...), custom_call_target="tpu_custom_call", output_to_operand_aliasing={{0}: (15, {})} | custom-call | flops 8589934592 | bytes 16777216 | tf_op jit(solution)/shard_map/pallas_call | solution.py:132
  1406.1 57.1 %psum.31 = f32[2,4,384]{2,1,0:T(4,128)S(1)} all-reduce(f32[2,4,384]{2,1,0:T(4,128)S(1)} %pad_maximum_fusion), channel_id=1, replica_groups=mesh['grp'=2,'seq'=8,'chan'=2] {'seq'}, use_global_device_ids=true, to_apply=%region_6.7 | all-reduce | flops 3072 | bytes 24576 | tf_op jit(solution)/shard_map/psum | solution.py:267
  1463.8 56.5 %all-reduce.10.cloned.1.call-done = (f32[256,256]{1,0:T(8,128)}, f32[512,512]{1,0:T(8,128)}) async-done(((f32[256,256]{1,0:T(8,128)}, f32[512,512]{1,0:T(8,128)}), (f32[256,256]{1,0:T(8,128)}, f32[512,512]{1,0:T(8,128)})) %all-reduce.10.cloned.1.call-update) | async-done | bytes 1310736 | tf_op jit(solution)/shard_map/psum | solution.py:268
  1524.3 79.3 %all-reduce.8.cloned.1.call-done = f32[768,384]{1,0:T(8,128)} async-done(((f32[768,384]{1,0:T(8,128)}), f32[768,384]{1,0:T(8,128)}) %all-reduce.8.cloned.1.call-update) | async-done | bytes 1179664 | tf_op jit(solution)/shard_map/psum | solution.py:235
  (286 shorter events, 142.3 us)
Async XLA Ops:
  7.2 819.7 %all-gather.5.cloned.1.call-start = ((), (), s32[]{:S(2)}) async-start(), calls=%async_computation.1 | async-start | bytes 1769472 | tf_op jit(solution)/shard_map/all_gather | solution.py:178
  14.6 19.1 %copy-start.1 = (f32[2,4,384]{2,1,0:T(4,128)S(1)}, f32[2,4,384]{2,1,0:T(4,128)}, u32[]{:S(2)}) copy-start(f32[2,4,384]{2,1,0:T(4,128)} %refs_12_.5) | copy-start | bytes 36868
  14.6 19.2 %copy-start.13 = (f32[64,256]{1,0:T(8,128)S(1)}, f32[64,256]{1,0:T(8,128)}, u32[]{:S(2)}) copy-start(f32[64,256]{1,0:T(8,128)} %param.11) | copy-start | bytes 196612
  16.4 128.0 %collective-permute-start.1 = (bf16[64,32,384]{2,0,1:T(8,128)(2,1)}, bf16[64,32,384]{2,0,1:T(8,128)(2,1)}, u32[]{:S(2)}, u32[]{:S(2)}) collective-permute-start(bf16[64,32,384]{2,0,1:T(8,128)(2,1)} %copy.211), channel_id=1, source_target_pairs={{0,2},{2,4},{4,6},{6,8},{8,10},{10,12},{12,14},{14,0},{1,3},{3,5},... | collective-permute-start | bytes 4718600 | tf_op jit(solution)/shard_map/ppermute | solution.py:31
  21.0 292.8 %collective-permute-start.2 = (bf16[64,32,384]{2,0,1:T(8,128)(2,1)}, bf16[64,32,384]{2,0,1:T(8,128)(2,1)}, u32[]{:S(2)}, u32[]{:S(2)}) collective-permute-start(bf16[64,32,384]{2,0,1:T(8,128)(2,1)} %copy.212), channel_id=1, source_target_pairs={{0,4},{2,6},{4,8},{6,10},{8,12},{10,14},{12,0},{14,2},{1,5},{3,7},... | collective-permute-start | bytes 4718600 | tf_op jit(solution)/shard_map/ppermute | solution.py:31
  24.3 304.7 %collective-permute-start.3 = (bf16[64,32,384]{2,0,1:T(8,128)(2,1)}, bf16[64,32,384]{2,0,1:T(8,128)(2,1)}, u32[]{:S(2)}, u32[]{:S(2)}) collective-permute-start(bf16[64,32,384]{2,0,1:T(8,128)(2,1)} %copy.213), channel_id=1, source_target_pairs={{0,6},{2,8},{4,10},{6,12},{8,14},{10,0},{12,2},{14,4},{1,7},{3,9},... | collective-permute-start | bytes 4718600 | tf_op jit(solution)/shard_map/ppermute | solution.py:31
  28.6 300.4 %collective-permute-start.4 = (bf16[64,32,384]{2,0,1:T(8,128)(2,1)}, bf16[64,32,384]{2,0,1:T(8,128)(2,1)}, u32[]{:S(2)}, u32[]{:S(2)}) collective-permute-start(bf16[64,32,384]{2,0,1:T(8,128)(2,1)} %copy.214), channel_id=1, source_target_pairs={{0,8},{2,10},{4,12},{6,14},{8,0},{10,2},{12,4},{14,6},{1,9},{3,11}... | collective-permute-start | bytes 4718600 | tf_op jit(solution)/shard_map/ppermute | solution.py:31
  31.1 22.2 %collective-permute-start = (bf16[3,384]{1,0:T(4,128)(2,1)S(1)}, bf16[3,384]{1,0:T(4,128)(2,1)S(1)}, u32[]{:S(2)}, u32[]{:S(2)}) collective-permute-start(bf16[3,384]{1,0:T(4,128)(2,1)S(1)} %get-tuple-element.60), channel_id=1, source_target_pairs={{0,2},{2,4},{4,6},{6,8},{8,10},{10,12},{12,14},{1,3},{3,5},{5,7},{... | collective-permute-start | bytes 6920 | tf_op jit(solution)/shard_map/ppermute | solution.py:16
  33.6 793.2 %all-gather.3.cloned.1.call-start = ((), (), s32[]{:S(2)}) async-start(), calls=%async_computation | async-start | bytes 37748736 | tf_op jit(solution)/shard_map/all_gather | solution.py:196
  33.8 71.4 %copy-start.14 = (f32[384]{0:T(512)}, f32[384]{0:T(512)S(1)}, u32[]{:S(2)}) copy-start(f32[384]{0:T(512)S(1)} %get-tuple-element.44) | copy-start | bytes 4612
  33.8 71.4 %copy-start.16 = (f32[384]{0:T(512)}, f32[384]{0:T(512)S(1)}, u32[]{:S(2)}) copy-start(f32[384]{0:T(512)S(1)} %get-tuple-element.45) | copy-start | bytes 4612
  33.8 71.4 %copy-start.18 = (f32[384]{0:T(512)}, f32[384]{0:T(512)S(1)}, u32[]{:S(2)}) copy-start(f32[384]{0:T(512)S(1)} %get-tuple-element.46) | copy-start | bytes 4612
  33.8 71.4 %copy-start.20 = (f32[384]{0:T(512)}, f32[384]{0:T(512)S(1)}, u32[]{:S(2)}) copy-start(f32[384]{0:T(512)S(1)} %get-tuple-element.47) | copy-start | bytes 4612
  33.8 71.4 %copy-start.22 = (f32[384]{0:T(512)}, f32[384]{0:T(512)S(1)}, u32[]{:S(2)}) copy-start(f32[384]{0:T(512)S(1)} %get-tuple-element.48) | copy-start | bytes 4612
  53.3 275.7 %collective-permute-start.5 = (bf16[64,32,384]{2,0,1:T(8,128)(2,1)}, bf16[64,32,384]{2,0,1:T(8,128)(2,1)S(1)}, u32[]{:S(2)}, u32[]{:S(2)}) collective-permute-start(bf16[64,32,384]{2,0,1:T(8,128)(2,1)} %copy.215), channel_id=1, source_target_pairs={{0,10},{2,12},{4,14},{6,0},{8,2},{10,4},{12,6},{14,8},{1,11},{3,13... | collective-permute-start | bytes 4718600 | tf_op jit(solution)/shard_map/ppermute | solution.py:31
  105.2 211.1 %copy-start.10 = (bf16[256,256]{1,0:T(8,128)(2,1)S(1)}, bf16[256,256]{1,0:T(8,128)(2,1)}, u32[]{:S(2)}) copy-start(bf16[256,256]{1,0:T(8,128)(2,1)} %param.10) | copy-start | bytes 393220
  144.4 204.7 %collective-permute-start.6 = (bf16[64,32,384]{2,0,1:T(8,128)(2,1)}, bf16[64,32,384]{2,0,1:T(8,128)(2,1)}, u32[]{:S(2)}, u32[]{:S(2)}) collective-permute-start(bf16[64,32,384]{2,0,1:T(8,128)(2,1)} %copy.216), channel_id=1, source_target_pairs={{0,12},{2,14},{4,0},{6,2},{8,4},{10,6},{12,8},{14,10},{1,13},{3,15... | collective-permute-start | bytes 4718600 | tf_op jit(solution)/shard_map/ppermute | solution.py:31
  313.9 66.5 %collective-permute-start.7 = (bf16[64,32,384]{2,0,1:T(8,128)(2,1)}, bf16[64,32,384]{2,0,1:T(8,128)(2,1)}, u32[]{:S(2)}, u32[]{:S(2)}) collective-permute-start(bf16[64,32,384]{2,0,1:T(8,128)(2,1)} %copy.217), channel_id=1, source_target_pairs={{0,14},{2,0},{4,2},{6,4},{8,6},{10,8},{12,10},{14,12},{1,15},{3,1}... | collective-permute-start | bytes 4718600 | tf_op jit(solution)/shard_map/ppermute | solution.py:31
  399.3 1121.0 %all-reduce.10.cloned.1.call-start = ((), (), s32[]{:S(2)}) async-start(), calls=%async_computation.3 | async-start | bytes 2621440 | tf_op jit(solution)/shard_map/psum | solution.py:268
  449.8 107.7 %copy-start.11 = (bf16[256,256]{1,0:T(8,128)(2,1)S(1)}, bf16[256,256]{1,0:T(8,128)(2,1)}, u32[]{:S(2)}) copy-start(bf16[256,256]{1,0:T(8,128)(2,1)} %param.10) | copy-start | bytes 393220
  449.8 160.5 %collective-permute-start.32 = (bf16[64,32,384]{2,1,0:T(8,128)(2,1)}, bf16[64,32,384]{2,1,0:T(8,128)(2,1)S(1)}, u32[]{:S(2)}, u32[]{:S(2)}) collective-permute-start(bf16[64,32,384]{2,1,0:T(8,128)(2,1)} %copy.180), channel_id=1, source_target_pairs={{0,2},{2,4},{4,6},{6,8},{8,10},{10,12},{12,14},{14,0},{1,3},{3,5},... | collective-permute-start | bytes 4718600 | tf_op jit(solution)/shard_map/ppermute | solution.py:31
  456.2 155.7 %collective-permute-start.33 = (bf16[64,32,384]{2,1,0:T(8,128)(2,1)}, bf16[64,32,384]{2,1,0:T(8,128)(2,1)}, u32[]{:S(2)}, u32[]{:S(2)}) collective-permute-start(bf16[64,32,384]{2,1,0:T(8,128)(2,1)} %copy.181), channel_id=1, source_target_pairs={{0,4},{2,6},{4,8},{6,10},{8,12},{10,14},{12,0},{14,2},{1,5},{3,7},... | collective-permute-start | bytes 4718600 | tf_op jit(solution)/shard_map/ppermute | solution.py:31
  567.5 49.5 %copy-start.9 = (bf16[512,256]{0,1:T(8,128)(2,1)}, bf16[512,256]{0,1:T(8,128)(2,1)S(1)}, u32[]{:S(2)}) copy-start(bf16[512,256]{0,1:T(8,128)(2,1)S(1)} %concatenate.80) | copy-start | bytes 786436
  580.4 98.6 %collective-permute-start.34 = (bf16[64,32,384]{2,1,0:T(8,128)(2,1)}, bf16[64,32,384]{2,1,0:T(8,128)(2,1)}, u32[]{:S(2)}, u32[]{:S(2)}) collective-permute-start(bf16[64,32,384]{2,1,0:T(8,128)(2,1)} %copy.182), channel_id=1, source_target_pairs={{0,6},{2,8},{4,10},{6,12},{8,14},{10,0},{12,2},{14,4},{1,7},{3,9},... | collective-permute-start | bytes 4718600 | tf_op jit(solution)/shard_map/ppermute | solution.py:31
  587.0 124.2 %collective-permute-start.35 = (bf16[64,32,384]{2,1,0:T(8,128)(2,1)}, bf16[64,32,384]{2,1,0:T(8,128)(2,1)}, u32[]{:S(2)}, u32[]{:S(2)}) collective-permute-start(bf16[64,32,384]{2,1,0:T(8,128)(2,1)} %copy.183), channel_id=1, source_target_pairs={{0,8},{2,10},{4,12},{6,14},{8,0},{10,2},{12,4},{14,6},{1,9},{3,11}... | collective-permute-start | bytes 4718600 | tf_op jit(solution)/shard_map/ppermute | solution.py:31
  593.7 123.8 %collective-permute-start.36 = (bf16[64,32,384]{2,1,0:T(8,128)(2,1)}, bf16[64,32,384]{2,1,0:T(8,128)(2,1)}, u32[]{:S(2)}, u32[]{:S(2)}) collective-permute-start(bf16[64,32,384]{2,1,0:T(8,128)(2,1)} %copy.184), channel_id=1, source_target_pairs={{0,10},{2,12},{4,14},{6,0},{8,2},{10,4},{12,6},{14,8},{1,11},{3,13... | collective-permute-start | bytes 4718600 | tf_op jit(solution)/shard_map/ppermute | solution.py:31
  603.9 14.4 copy-start.15
  603.9 14.4 copy-start.17
  603.9 14.5 copy-start.19
  603.9 14.5 copy-start.21
  603.9 14.5 copy-start.23
  610.3 113.5 %collective-permute-start.37 = (bf16[64,32,384]{2,1,0:T(8,128)(2,1)}, bf16[64,32,384]{2,1,0:T(8,128)(2,1)}, u32[]{:S(2)}, u32[]{:S(2)}) collective-permute-start(bf16[64,32,384]{2,1,0:T(8,128)(2,1)} %copy.185), channel_id=1, source_target_pairs={{0,12},{2,14},{4,0},{6,2},{8,4},{10,6},{12,8},{14,10},{1,13},{3,15... | collective-permute-start | bytes 4718600 | tf_op jit(solution)/shard_map/ppermute | solution.py:31
  611.9 130.9 %collective-permute-start.38 = (bf16[64,32,384]{2,1,0:T(8,128)(2,1)}, bf16[64,32,384]{2,1,0:T(8,128)(2,1)}, u32[]{:S(2)}, u32[]{:S(2)}) collective-permute-start(bf16[64,32,384]{2,1,0:T(8,128)(2,1)} %copy.186), channel_id=1, source_target_pairs={{0,14},{2,0},{4,2},{6,4},{8,6},{10,8},{12,10},{14,12},{1,15},{3,1}... | collective-permute-start | bytes 4718600 | tf_op jit(solution)/shard_map/ppermute | solution.py:31
  903.4 93.2 %copy-start.3 = (bf16[512,32,128]{2,1,0:T(8,128)(2,1)}, bf16[512,32,128]{2,1,0:T(8,128)(2,1)S(1)}, u32[]{:S(2)}) copy-start(bf16[512,32,128]{2,1,0:T(8,128)(2,1)S(1)} %get-tuple-element.111) | copy-start | bytes 12582916
  903.4 93.2 %copy-start.5 = (bf16[512,32,128]{2,1,0:T(8,128)(2,1)}, bf16[512,32,128]{2,1,0:T(8,128)(2,1)S(1)}, u32[]{:S(2)}) copy-start(bf16[512,32,128]{2,1,0:T(8,128)(2,1)S(1)} %get-tuple-element.113) | copy-start | bytes 12582916
  903.5 93.1 %copy-start.4 = (bf16[512,32,128]{2,1,0:T(8,128)(2,1)}, bf16[512,32,128]{2,1,0:T(8,128)(2,1)S(1)}, u32[]{:S(2)}) copy-start(bf16[512,32,128]{2,1,0:T(8,128)(2,1)S(1)} %get-tuple-element.112) | copy-start | bytes 12582916
  905.9 127.3 %collective-permute-start.24 = (bf16[64,32,128]{2,1,0:T(8,128)(2,1)}, bf16[64,32,128]{2,1,0:T(8,128)(2,1)S(1)}, u32[]{:S(2)}, u32[]{:S(2)}) collective-permute-start(bf16[64,32,128]{2,1,0:T(8,128)(2,1)} %get-tuple-element.75), channel_id=1, source_target_pairs={{0,2},{2,4},{4,6},{6,8},{8,10},{10,12},{12,14},{14,0},{1,3},{3,5},... | collective-permute-start | bytes 1572872 | tf_op jit(solution)/shard_map/ppermute | solution.py:31
  922.0 111.1 %collective-permute-start.25 = (bf16[64,32,128]{2,1,0:T(8,128)(2,1)}, bf16[64,32,128]{2,1,0:T(8,128)(2,1)S(1)}, u32[]{:S(2)}, u32[]{:S(2)}) collective-permute-start(bf16[64,32,128]{2,1,0:T(8,128)(2,1)} %get-tuple-element.74), channel_id=1, source_target_pairs={{0,4},{2,6},{4,8},{6,10},{8,12},{10,14},{12,0},{14,2},{1,5},{3,7},... | collective-permute-start | bytes 1572872 | tf_op jit(solution)/shard_map/ppermute | solution.py:31
  985.9 53.7 %collective-permute-start.26 = (bf16[64,32,128]{2,1,0:T(8,128)(2,1)}, bf16[64,32,128]{2,1,0:T(8,128)(2,1)S(1)}, u32[]{:S(2)}, u32[]{:S(2)}) collective-permute-start(bf16[64,32,128]{2,1,0:T(8,128)(2,1)} %get-tuple-element.73), channel_id=1, source_target_pairs={{0,6},{2,8},{4,10},{6,12},{8,14},{10,0},{12,2},{14,4},{1,7},{3,9},... | collective-permute-start | bytes 1572872 | tf_op jit(solution)/shard_map/ppermute | solution.py:31
  985.9 54.0 %collective-permute-start.27 = (bf16[64,32,128]{2,1,0:T(8,128)(2,1)}, bf16[64,32,128]{2,1,0:T(8,128)(2,1)}, u32[]{:S(2)}, u32[]{:S(2)}) collective-permute-start(bf16[64,32,128]{2,1,0:T(8,128)(2,1)} %get-tuple-element.72), channel_id=1, source_target_pairs={{0,8},{2,10},{4,12},{6,14},{8,0},{10,2},{12,4},{14,6},{1,9},{3,11}... | collective-permute-start | bytes 1572872 | tf_op jit(solution)/shard_map/ppermute | solution.py:31
  991.2 75.6 %collective-permute-start.28 = (bf16[64,32,128]{2,1,0:T(8,128)(2,1)}, bf16[64,32,128]{2,1,0:T(8,128)(2,1)}, u32[]{:S(2)}, u32[]{:S(2)}) collective-permute-start(bf16[64,32,128]{2,1,0:T(8,128)(2,1)} %get-tuple-element.71), channel_id=1, source_target_pairs={{0,10},{2,12},{4,14},{6,0},{8,2},{10,4},{12,6},{14,8},{1,11},{3,13... | collective-permute-start | bytes 1572872 | tf_op jit(solution)/shard_map/ppermute | solution.py:31
  1003.5 265.2 %copy-start.2 = (f32[2,4,384]{2,1,0:T(4,128)S(1)}, f32[2,4,384]{2,1,0:T(4,128)}, u32[]{:S(2)}) copy-start(f32[2,4,384]{2,1,0:T(4,128)} %refs_12_.5) | copy-start | bytes 36868
  1033.1 36.4 %collective-permute-start.29 = (bf16[64,32,128]{2,1,0:T(8,128)(2,1)}, bf16[64,32,128]{2,1,0:T(8,128)(2,1)S(1)}, u32[]{:S(2)}, u32[]{:S(2)}) collective-permute-start(bf16[64,32,128]{2,1,0:T(8,128)(2,1)} %get-tuple-element.70), channel_id=1, source_target_pairs={{0,12},{2,14},{4,0},{6,2},{8,4},{10,6},{12,8},{14,10},{1,13},{3,15... | collective-permute-start | bytes 1572872 | tf_op jit(solution)/shard_map/ppermute | solution.py:31
  1033.2 225.1 %collective-permute-start.30 = (bf16[64,32,128]{2,1,0:T(8,128)(2,1)}, bf16[64,32,128]{2,1,0:T(8,128)(2,1)S(1)}, u32[]{:S(2)}, u32[]{:S(2)}) collective-permute-start(bf16[64,32,128]{2,1,0:T(8,128)(2,1)} %get-tuple-element.69), channel_id=1, source_target_pairs={{0,14},{2,0},{4,2},{6,4},{8,6},{10,8},{12,10},{14,12},{1,15},{3,1}... | collective-permute-start | bytes 1572872 | tf_op jit(solution)/shard_map/ppermute | solution.py:31
  1039.6 40.2 %collective-permute-start.8 = (bf16[64,32,128]{2,1,0:T(8,128)(2,1)}, bf16[64,32,128]{2,1,0:T(8,128)(2,1)S(1)}, u32[]{:S(2)}, u32[]{:S(2)}) collective-permute-start(bf16[64,32,128]{2,1,0:T(8,128)(2,1)} %get-tuple-element.91), channel_id=1, source_target_pairs={{0,2},{2,4},{4,6},{6,8},{8,10},{10,12},{12,14},{14,0},{1,3},{3,5},... | collective-permute-start | bytes 1572872 | tf_op jit(solution)/shard_map/ppermute | solution.py:31
  1040.0 69.1 %collective-permute-start.9 = (bf16[64,32,128]{2,1,0:T(8,128)(2,1)}, bf16[64,32,128]{2,1,0:T(8,128)(2,1)S(1)}, u32[]{:S(2)}, u32[]{:S(2)}) collective-permute-start(bf16[64,32,128]{2,1,0:T(8,128)(2,1)} %get-tuple-element.90), channel_id=1, source_target_pairs={{0,4},{2,6},{4,8},{6,10},{8,12},{10,14},{12,0},{14,2},{1,5},{3,7},... | collective-permute-start | bytes 1572872 | tf_op jit(solution)/shard_map/ppermute | solution.py:31
  1066.8 65.2 %collective-permute-start.10 = (bf16[64,32,128]{2,1,0:T(8,128)(2,1)}, bf16[64,32,128]{2,1,0:T(8,128)(2,1)S(1)}, u32[]{:S(2)}, u32[]{:S(2)}) collective-permute-start(bf16[64,32,128]{2,1,0:T(8,128)(2,1)} %get-tuple-element.89), channel_id=1, source_target_pairs={{0,6},{2,8},{4,10},{6,12},{8,14},{10,0},{12,2},{14,4},{1,7},{3,9},... | collective-permute-start | bytes 1572872 | tf_op jit(solution)/shard_map/ppermute | solution.py:31
  1069.5 62.5 %collective-permute-start.11 = (bf16[64,32,128]{2,1,0:T(8,128)(2,1)}, bf16[64,32,128]{2,1,0:T(8,128)(2,1)S(1)}, u32[]{:S(2)}, u32[]{:S(2)}) collective-permute-start(bf16[64,32,128]{2,1,0:T(8,128)(2,1)} %get-tuple-element.88), channel_id=1, source_target_pairs={{0,8},{2,10},{4,12},{6,14},{8,0},{10,2},{12,4},{14,6},{1,9},{3,11}... | collective-permute-start | bytes 1572872 | tf_op jit(solution)/shard_map/ppermute | solution.py:31
  1079.8 63.9 %collective-permute-start.12 = (bf16[64,32,128]{2,1,0:T(8,128)(2,1)}, bf16[64,32,128]{2,1,0:T(8,128)(2,1)S(1)}, u32[]{:S(2)}, u32[]{:S(2)}) collective-permute-start(bf16[64,32,128]{2,1,0:T(8,128)(2,1)} %get-tuple-element.87), channel_id=1, source_target_pairs={{0,10},{2,12},{4,14},{6,0},{8,2},{10,4},{12,6},{14,8},{1,11},{3,13... | collective-permute-start | bytes 1572872 | tf_op jit(solution)/shard_map/ppermute | solution.py:31
  1109.1 54.1 %collective-permute-start.13 = (bf16[64,32,128]{2,1,0:T(8,128)(2,1)}, bf16[64,32,128]{2,1,0:T(8,128)(2,1)S(1)}, u32[]{:S(2)}, u32[]{:S(2)}) collective-permute-start(bf16[64,32,128]{2,1,0:T(8,128)(2,1)} %get-tuple-element.86), channel_id=1, source_target_pairs={{0,12},{2,14},{4,0},{6,2},{8,4},{10,6},{12,8},{14,10},{1,13},{3,15... | collective-permute-start | bytes 1572872 | tf_op jit(solution)/shard_map/ppermute | solution.py:31
  1132.0 67.9 %collective-permute-start.14 = (bf16[64,32,128]{2,1,0:T(8,128)(2,1)}, bf16[64,32,128]{2,1,0:T(8,128)(2,1)S(1)}, u32[]{:S(2)}, u32[]{:S(2)}) collective-permute-start(bf16[64,32,128]{2,1,0:T(8,128)(2,1)} %get-tuple-element.85), channel_id=1, source_target_pairs={{0,14},{2,0},{4,2},{6,4},{8,6},{10,8},{12,10},{14,12},{1,15},{3,1}... | collective-permute-start | bytes 1572872 | tf_op jit(solution)/shard_map/ppermute | solution.py:31
  1132.0 67.9 %collective-permute-start.16 = (bf16[64,32,128]{2,1,0:T(8,128)(2,1)}, bf16[64,32,128]{2,1,0:T(8,128)(2,1)S(1)}, u32[]{:S(2)}, u32[]{:S(2)}) collective-permute-start(bf16[64,32,128]{2,1,0:T(8,128)(2,1)} %get-tuple-element.83), channel_id=1, source_target_pairs={{0,2},{2,4},{4,6},{6,8},{8,10},{10,12},{12,14},{14,0},{1,3},{3,5},... | collective-permute-start | bytes 1572872 | tf_op jit(solution)/shard_map/ppermute | solution.py:31
  1143.7 56.2 %collective-permute-start.17 = (bf16[64,32,128]{2,1,0:T(8,128)(2,1)}, bf16[64,32,128]{2,1,0:T(8,128)(2,1)S(1)}, u32[]{:S(2)}, u32[]{:S(2)}) collective-permute-start(bf16[64,32,128]{2,1,0:T(8,128)(2,1)} %get-tuple-element.82), channel_id=1, source_target_pairs={{0,4},{2,6},{4,8},{6,10},{8,12},{10,14},{12,0},{14,2},{1,5},{3,7},... | collective-permute-start | bytes 1572872 | tf_op jit(solution)/shard_map/ppermute | solution.py:31
  1163.2 60.0 %collective-permute-start.18 = (bf16[64,32,128]{2,1,0:T(8,128)(2,1)}, bf16[64,32,128]{2,1,0:T(8,128)(2,1)S(1)}, u32[]{:S(2)}, u32[]{:S(2)}) collective-permute-start(bf16[64,32,128]{2,1,0:T(8,128)(2,1)} %get-tuple-element.81), channel_id=1, source_target_pairs={{0,6},{2,8},{4,10},{6,12},{8,14},{10,0},{12,2},{14,4},{1,7},{3,9},... | collective-permute-start | bytes 1572872 | tf_op jit(solution)/shard_map/ppermute | solution.py:31
  1199.9 36.4 %collective-permute-start.19 = (bf16[64,32,128]{2,1,0:T(8,128)(2,1)}, bf16[64,32,128]{2,1,0:T(8,128)(2,1)S(1)}, u32[]{:S(2)}, u32[]{:S(2)}) collective-permute-start(bf16[64,32,128]{2,1,0:T(8,128)(2,1)} %get-tuple-element.80), channel_id=1, source_target_pairs={{0,8},{2,10},{4,12},{6,14},{8,0},{10,2},{12,4},{14,6},{1,9},{3,11}... | collective-permute-start | bytes 1572872 | tf_op jit(solution)/shard_map/ppermute | solution.py:31
  1199.9 36.4 %collective-permute-start.20 = (bf16[64,32,128]{2,1,0:T(8,128)(2,1)}, bf16[64,32,128]{2,1,0:T(8,128)(2,1)S(1)}, u32[]{:S(2)}, u32[]{:S(2)}) collective-permute-start(bf16[64,32,128]{2,1,0:T(8,128)(2,1)} %get-tuple-element.79), channel_id=1, source_target_pairs={{0,10},{2,12},{4,14},{6,0},{8,2},{10,4},{12,6},{14,8},{1,11},{3,13... | collective-permute-start | bytes 1572872 | tf_op jit(solution)/shard_map/ppermute | solution.py:31
  1200.0 46.2 %collective-permute-start.21 = (bf16[64,32,128]{2,1,0:T(8,128)(2,1)}, bf16[64,32,128]{2,1,0:T(8,128)(2,1)S(1)}, u32[]{:S(2)}, u32[]{:S(2)}) collective-permute-start(bf16[64,32,128]{2,1,0:T(8,128)(2,1)} %get-tuple-element.78), channel_id=1, source_target_pairs={{0,12},{2,14},{4,0},{6,2},{8,4},{10,6},{12,8},{14,10},{1,13},{3,15... | collective-permute-start | bytes 1572872 | tf_op jit(solution)/shard_map/ppermute | solution.py:31
  1223.2 33.3 %collective-permute-start.22 = (bf16[64,32,128]{2,1,0:T(8,128)(2,1)}, bf16[64,32,128]{2,1,0:T(8,128)(2,1)S(1)}, u32[]{:S(2)}, u32[]{:S(2)}) collective-permute-start(bf16[64,32,128]{2,1,0:T(8,128)(2,1)} %get-tuple-element.77), channel_id=1, source_target_pairs={{0,14},{2,0},{4,2},{6,4},{8,6},{10,8},{12,10},{14,12},{1,15},{3,1}... | collective-permute-start | bytes 1572872 | tf_op jit(solution)/shard_map/ppermute | solution.py:31
  1259.3 6.6 collective-permute-start.31
  1260.6 6.1 collective-permute-start.23
  1261.9 6.8 collective-permute-start.15
  1265.8 137.8 %collective-permute-start.39 = (f32[384,384]{1,0:T(8,128)}, f32[384,384]{1,0:T(8,128)}, u32[]{:S(2)}, u32[]{:S(2)}) collective-permute-start(f32[384,384]{1,0:T(8,128)} %get-tuple-element.102), channel_id=1, source_target_pairs={{0,1},{1,0},{2,3},{3,2},{4,5},{5,4},{6,7},{7,6},{8,9},{9,8},{10,11... | collective-permute-start | bytes 1769480 | tf_op jit(solution)/shard_map/ppermute | solution.py:231
  1359.6 44.0 %copy-start.7 = (f32[384,384]{1,0:T(8,128)S(1)}, f32[384,384]{1,0:T(8,128)}, u32[]{:S(2)}) copy-start(f32[384,384]{1,0:T(8,128)} %get-tuple-element.101) | copy-start | bytes 1769476
  1403.5 200.0 %all-reduce.8.cloned.1.call-start = ((), (), s32[]{:S(2)}) async-start(), calls=%async_computation.2 | async-start | bytes 2359296 | tf_op jit(solution)/shard_map/psum | solution.py:235
  (14 other events, 91.7 us)
Sparse Core Ops, SparseCore 0:
  33.8 8.4 all-gather.4
  399.4 54.9 all-gather.2
  1403.7 116.5 all-reduce.9
  1523.6 79.8 all-reduce.7

commit v2 on v1

v2 whole, which is shorter than its diff:
```python
import jax
import jax.numpy as jnp
from jax import lax
from jax.experimental import pallas as pl
from jax.experimental.pallas import tpu as pltpu
from jax.sharding import PartitionSpec as P


def passed_along(array, axis, by):
    peers = lax.axis_size(axis)
    pairs = [(i, i + by) for i in range(peers) if 0 <= i + by < peers]
    return lax.ppermute(array, axis, pairs)


def causal_taps(history_rows, weights, tokens):
    result = weights[0] * history_rows[3 : 3 + tokens]
    for offset in range(1, 4):
        result = result + weights[offset] * history_rows[3 - offset : 3 - offset + tokens]
    return result


def exchange(array):
    return lax.all_to_all(array, "seq", split_axis=0, concat_axis=0, tiled=True)


def tail_kernel(*refs):
    (grad_ref, twiddle_ref, inputs_ref, before_ref, last_ref) = refs[:5]
    (cot_ref, weight_ref, mix_ref, halo_ref) = refs[5:9]
    (out_ref, inner_ref, conv_ref) = refs[-6:-3]
    (signal, value_ext, gate_ext) = refs[-3:]
    step = pl.program_id(0)
    steps = pl.num_programs(0)
    rows = inputs_ref.shape[0]
    taps = weight_ref.shape[1]

    @pl.when(step == 0)
    def _():
        inner_ref[...] = jnp.zeros_like(inner_ref)
        conv_ref[...] = jnp.zeros_like(conv_ref)
        value_ext[0:8] = halo_ref[0]
        gate_ext[0:8] = halo_ref[1]

    value_ext[rows : rows + 8] = value_ext[0:8]
    gate_ext[rows : rows + 8] = gate_ext[0:8]
    signal[8 : 8 + rows] = inputs_ref[...].astype(jnp.float32)
    before = before_ref[...].astype(jnp.float32)[8:16]
    signal[0:8] = jnp.where(step == steps - 1, last_ref[...], before)
    weight = weight_ref[...]
    shifted = [signal[8 - s : 8 - s + rows] for s in range(taps)]
    value_conv = weight[0, 0][None] * shifted[0]
    gate_conv = weight[1, 0][None] * shifted[0]
    for s in range(1, taps):
        value_conv = value_conv + weight[0, s][None] * shifted[s]
        gate_conv = gate_conv + weight[1, s][None] * shifted[s]
    gate_sig = jax.nn.sigmoid(gate_conv)
    value_part = value_conv * gate_sig
    gated = value_part.astype(jnp.bfloat16)
    grad = grad_ref[:, 0].reshape(rows, -1).astype(jnp.float32)
    table = twiddle_ref[...]
    lane = lax.broadcasted_iota(jnp.int32, table.shape, 1)
    factor = jnp.sum(jnp.where(lane == steps - 1 - step, table, 0.0), 1, keepdims=True)
    grad = (grad * factor).astype(jnp.bfloat16)
    inner_ref[...] += lax.dot_general(
        grad, gated, (((1,), (1,)), ((), ())), preferred_element_type=jnp.float32
    )
    gated_grad = jnp.dot(mix_ref[...], grad, preferred_element_type=jnp.float32)
    value_grad = gated_grad * gate_sig
    gate_grad = gated_grad * value_part * (1.0 - gate_sig)
    value_ext[0:rows] = value_grad
    gate_ext[0:rows] = gate_grad
    for s in range(taps):
        conv_ref[0, s] += jnp.sum((value_grad * shifted[s]).reshape(rows // 8, 8, -1), 0)
        conv_ref[1, s] += jnp.sum((gate_grad * shifted[s]).reshape(rows // 8, 8, -1), 0)
    total = cot_ref[...].astype(jnp.float32)
    for s in range(taps):
        total = total + weight[0, s][None] * value_ext[s : s + rows]
        total = total + weight[1, s][None] * gate_ext[s : s + rows]
    out_ref[...] = total.astype(jnp.bfloat16)


def tail(grads, turned_twiddle, inputs, last_rows, cotangent, conv_weight, mix_turned, halo):
    tokens, channels = inputs.shape
    inner_size = mix_turned.shape[0]
    blocks = tokens // inner_size
    ratio = inner_size // 16

    def place(step):
        return blocks - 1 - step

    whole = pl.BlockSpec(memory_space=pltpu.VMEM)
    rows = pl.BlockSpec((inner_size, channels), lambda step: (place(step), 0))
    before = pl.BlockSpec(
        (16, channels), lambda step: (jnp.maximum(place(step) * ratio - 1, 0), 0)
    )
    grad_rows = pl.BlockSpec(
        (grads.shape[0], 1, grads.shape[2], channels), lambda step: (0, place(step), 0, 0)
    )
    return pl.pallas_call(
        tail_kernel,
        grid=(blocks,),
        in_specs=[grad_rows, whole, rows, before, whole, rows, whole, whole, whole],
        out_specs=[
            rows,
            pl.BlockSpec((inner_size, inner_size), lambda step: (0, 0)),
            pl.BlockSpec((2, 4, 8, channels), lambda step: (0, 0, 0, 0)),
        ],
        out_shape=[
            jax.ShapeDtypeStruct((tokens, channels), jnp.bfloat16),
            jax.ShapeDtypeStruct((inner_size, inner_size), jnp.float32),
            jax.ShapeDtypeStruct((2, 4, 8, channels), jnp.float32),
        ],
        scratch_shapes=[pltpu.VMEM((inner_size + 8, channels), jnp.float32)] * 3,
        compiler_params=pltpu.CompilerParams(vmem_limit_bytes=32 * 1024 * 1024),
        cost_estimate=pl.CostEstimate(
            flops=tokens * channels * inner_size * 4,
            bytes_accessed=tokens * channels * 8,
            transcendentals=tokens * channels,
        ),
    )(
        grads, turned_twiddle, inputs, inputs, last_rows, cotangent, conv_weight, mix_turned, halo
    )


def body(inputs, cotangent, conv_weight, mix_inner, twiddle, mix_outer, proj_weight):
    peers = lax.axis_size("seq")
    half = lax.axis_index("chan")
    halves = lax.axis_size("chan")
    inner_size = mix_inner.shape[0]
    outer_size = mix_outer.shape[0]
    tokens, channels = inputs.shape
    blocks = tokens // inner_size
    cols = inner_size // peers
    grad_scale = (outer_size * inner_size) ** (-0.5)
    swap = [(i, halves - 1 - i) for i in range(halves)]

    def by_owner(array):
        turned = array.reshape(blocks, peers, cols, channels).transpose(1, 0, 2, 3)
        return turned.reshape(peers * blocks, cols, channels)

    cot_turned = exchange(by_owner(cotangent))
    last_rows = passed_along(inputs[tokens - 3 :], "seq", 1)
    weight_all = lax.all_gather(proj_weight, "chan", axis=1)
    weight_rows = lax.dynamic_slice_in_dim(weight_all, half * channels, channels, 0)

    history_rows = jnp.concatenate([last_rows, inputs], 0).astype(jnp.float32)
    value_conv = causal_taps(history_rows, conv_weight[0], tokens)
    gate_conv = causal_taps(history_rows, conv_weight[1], tokens)
    gated_input = (value_conv * jax.nn.sigmoid(gate_conv)).astype(jnp.bfloat16)
    gated_blocks = gated_input.reshape(blocks, inner_size, channels)
    inner_mixed = jnp.einsum(
        "kj,ijc->ikc", mix_inner, gated_blocks, preferred_element_type=jnp.float32
    )
    twisted = (inner_mixed * twiddle[:, :, None]).astype(jnp.bfloat16)
    sent = by_owner(twisted)
    sent, cot_turned = lax.optimization_barrier((sent, cot_turned))
    received = exchange(sent)

    cot_wide = lax.all_gather(cot_turned, "chan", axis=0)
    mixed_grad = jnp.einsum(
        "hmkd,chd->mkc", cot_wide, weight_rows, preferred_element_type=jnp.float32
    ).astype(jnp.bfloat16)
    twisted_grad = jnp.einsum(
        "mi,mkc->ikc", mix_outer, mixed_grad, preferred_element_type=jnp.float32
    ).astype(jnp.bfloat16)
    twisted_grad, received = lax.optimization_barrier((twisted_grad, received))
    grads = exchange(twisted_grad).reshape(peers, blocks, cols, channels)

    mixed = jnp.einsum(
        "mi,ikc->mkc", mix_outer, received, preferred_element_type=jnp.float32
    ).astype(jnp.bfloat16)
    outer_part = jnp.einsum(
        "mkc,ikc->mi", mixed_grad, received, preferred_element_type=jnp.float32
    )
    proj_part = jnp.einsum(
        "mkc,hmkd->hcd", mixed, cot_wide, preferred_element_type=jnp.float32
    )
    own = lax.dynamic_index_in_dim(proj_part, half, 0, keepdims=False)
    other = lax.dynamic_index_in_dim(proj_part, halves - 1 - half, 0, keepdims=False)
    other, outer_other = lax.ppermute((other, outer_part), "chan", swap)
    proj_part = jnp.where(
        half == 0, jnp.concatenate([own, other], 0), jnp.concatenate([other, own], 0)
    )
    proj_sum, outer_sum = lax.psum((proj_part, outer_part + outer_other), "seq")

    pad_rows = jnp.concatenate([jnp.zeros((5, channels), jnp.bfloat16), last_rows], 0)
    pad_rows = pad_rows.astype(jnp.float32)
    first_history = jnp.concatenate([last_rows, inputs[:3]], 0).astype(jnp.float32)
    first_value = causal_taps(first_history, conv_weight[0], 3)
    sig = jax.nn.sigmoid(causal_taps(first_history, conv_weight[1], 3))
    first = grads[:, 0].reshape(inner_size, channels).astype(jnp.float32)
    first = (first * twiddle[0][:, None]).astype(jnp.bfloat16)
    first_grad = lax.dot_general(
        mix_inner[:, :3], first, (((0,), (0,)), ((), ())), preferred_element_type=jnp.float32
    )
    edge = jnp.stack([first_grad * sig, first_grad * first_value * sig * (1.0 - sig)])
    halo = passed_along(edge, "seq", -1)
    halo = jnp.concatenate([halo, jnp.zeros((2, 5, channels), jnp.float32)], 1)
    if cols % 16:
        grads = grads.transpose(1, 0, 2, 3).reshape(1, blocks, inner_size, channels)
    result, inner_part, conv_part = tail(
        grads, twiddle.T, inputs, pad_rows, cotangent, conv_weight, mix_inner.T, halo
    )
    conv_part = jnp.sum(conv_part, 2).reshape(1, -1)
    mine = (jnp.arange(halves) == half)[:, None]
    conv_both = jnp.where(mine, conv_part, 0.0)
    flat = jnp.concatenate([inner_part.reshape(-1), conv_both.reshape(-1)])
    flat = lax.psum(flat, ("seq", "chan"))
    inner_sum = flat[: inner_size * inner_size].reshape(inner_size, inner_size)
    conv_both = flat[inner_size * inner_size :].reshape(halves, *conv_weight.shape)
    conv_sum = lax.dynamic_index_in_dim(conv_both, half, 0, keepdims=False)
    return (
        result,
        (proj_sum * grad_scale).astype(jnp.bfloat16),
        inner_sum * grad_scale,
        outer_sum * grad_scale,
        conv_sum * grad_scale,
    )


def solution(mesh):
    in_specs = (
        P(("grp", "seq"), "chan"),
        P(("grp", "seq"), "chan"),
        P(None, None, "chan"),
        P(),
        P("seq", None),
        P(),
        P(None, "chan"),
    )
    out_specs = (
        P(("grp", "seq"), "chan"),
        P("grp", "chan"),
        P("grp", None),
        P("grp", None),
        P("grp", None, "chan"),
    )
    return jax.shard_map(body, mesh=mesh, in_specs=in_specs, out_specs=out_specs, check_vma=False)
```

time: 1630 us -> 1230 us (0.75); the launches traced: 1610 us -> 1230 us
  waiting for transfers between devices: 366 us -> 794 us
  starting transfers between devices: 478 us -> 103 us
  local copies, waits for them, and re-layouts: 307 us -> 68.1 us
  blocking collectives: 140 us -> 0 us
  Pallas kernels: 129 us -> 91.7 us
  other arithmetic: 90.7 us -> 66.3 us
    all_to_all x0 -> x3, waiting for transfers between devices: none -> 522 us  [exchange(): return lax.all_to_all(array, 'seq', split_axis=0, concat_axis=0, tiled=True)]
    ppermute x36 -> x2, starting transfers between devices: 471 us -> 0.56 us  [body(): other, outer_other = lax.ppermute((other, outer_part), 'chan', swap)]
    ppermute x36 -> x2, waiting for transfers between devices: 218 us -> 1.84 us  [body(): other, outer_other = lax.ppermute((other, outer_part), 'chan', swap)]
    all_to_all x0 -> x3, starting transfers between devices: none -> 97.1 us  [exchange(): return lax.all_to_all(array, 'seq', split_axis=0, concat_axis=0, tiled=True)]
    slice x14 -> x4, local copies, waits for them, and re-layouts: 95.8 us -> 1.69 us  [the longest x1 0.95 us: body(): first = grads[:, 0].reshape(inner_size, channels).astype(jnp.float32)]
    unnamed x169 -> x37, local copies, waits for them, and re-layouts: 90.5 us -> 1.49 us
    ppermute x4 -> x2, waiting for transfers between devices: 12.1 us -> 96.1 us  [passed_along(): return lax.ppermute(array, axis, pairs)]
    all_gather x1 -> x0, blocking collectives: 82.6 us -> none  [body(): twiddle_all = lax.all_gather(twiddle, 'seq', axis=0, tiled=True)]
  transfers between devices with their start and end apart: 44 -> 11, of which waited for: 17 -> 8; matrix products, arithmetic and copies ran while one was open for 24% -> 16% of each run, Pallas kernels for 8% -> 0%
where the time goes in v2:
time: 1230 us
  waiting for transfers between devices  794 us (65%)
  starting transfers between devices  103 us (8%)
  matrix products  95.2 us (8%)
  Pallas kernels  91.7 us (7%)
  local copies, waits for them, and re-layouts  68.1 us (6%)
  other arithmetic  66.3 us (5%)
  between operations  14.1 us (1%)
    all_to_all x3, waiting for transfers between devices, exchange(): return lax.all_to_all(array, 'seq', split_axis=0, concat_axis=0, tiled=True)  522 us
    all_to_all x3, starting transfers between devices, exchange(): return lax.all_to_all(array, 'seq', split_axis=0, concat_axis=0, tiled=True)  97.1 us
    ppermute x2, waiting for transfers between devices, passed_along(): return lax.ppermute(array, axis, pairs)  96.1 us
    pallas_call x1, Pallas kernels, tail(): pl.pallas_call(tail_kernel, grid=(blocks,), in_specs=[grad_rows, whole, r...  91.7 us
    psum x1, waiting for transfers between devices, body(): flat = lax.psum(flat, ('seq', 'chan'))  88.3 us
    psum x1, waiting for transfers between devices, body(): proj_sum, outer_sum = lax.psum((proj_part, outer_part + outer_other), 'seq')  51.1 us
    convert_element_type x1, other arithmetic, body(): gated_input = (value_conv * jax.nn.sigmoid(gate_conv)).astype(jnp.bfloat16)  40 us
    all_gather x1, waiting for transfers between devices, body(): cot_wide = lax.all_gather(cot_turned, 'chan', axis=0)  34.4 us
  transfers between devices with their start and end apart: 11, of which 8 were waited for; matrix products, arithmetic and copies ran while one was open for 16% of the time, Pallas kernels for 0%

profile of v2, /device:TPU:0, one launch (start us, length us, event | category | flops | bytes accessed | tf_op | source)
XLA Modules:
  0.0 1232.5 jit_solution(3921176170340590973)
XLA Ops:
  7.2 0.0 copy-start
  7.2 11.2 copy.40
  18.4 7.4 all-to-all-start
  25.8 0.0 all-gather.5.cloned.1.call-start
  25.9 1.3 fusion.30
  27.2 3.9 collective-permute-start
  31.2 96.1 %collective-permute-done = bf16[3,384]{1,0:T(4,128)(2,1)S(1)} collective-permute-done((bf16[3,384]{1,0:T(4,128)(2,1)S(1)}, bf16[3,384]{1,0:T(4,128)(2,1)S(1)}, u32[]{:S(2)}, u32[]{:S(2)}) %collective-permute-start) | collective-permute-done | bytes 2336 | tf_op jit(solution)/shard_map/ppermute | solution.py:12
  127.2 14.2 %maximum_convert_fusion = f32[16387,384]{1,0:T(8,128)} fusion(bf16[16384,384]{1,0:T(8,128)(2,1)} %refs_3_.1, bf16[3,384]{1,0:T(4,128)(2,1)S(1)} %collective-permute-done), kind=kLoop, calls=%fused_computation.3 | loop fusion | flops 25170432 | bytes 37755648 | tf_op jit(solution)/shard_map/convert_element_type | solution.py:145
  141.5 0.0 copy-start.4
  141.5 0.0 copy-start.6
  141.5 40.0 %multiply_convert_fusion.1 = bf16[16384,384]{1,0:T(8,128)(2,1)} fusion(f32[16387,384]{1,0:T(8,128)} %maximum_convert_fusion, f32[384]{0:T(512)S(1)} %get-tuple-element.26, f32[384]{0:T(512)S(1)} %get-tuple-element.20, f32[384]{0:T(512)S(1)} %get-tuple-element.21, f32[384]{0:T(512)S(1)} %get-tuple-element.22, f32[384]{0:T(512)S(1)} %get-tuple-element.23, ...), kind=kLoop, calls=%fused_computation.2 | loop fusion | flops 119537664 | bytes 113258496 | tf_op jit(solution)/shard_map/convert_element_type | solution.py:148
  181.6 15.9 %multiply_convert_fusion = bf16[64,384,256]{1,2,0:T(8,128)(2,1)} fusion(f32[64,256]{1,0:T(8,128)S(1)} %copy-done.4, bf16[64,256,384]{2,1,0:T(8,128)(2,1)} %bitcast.80, bf16[256,256]{1,0:T(8,128)(2,1)S(1)} %copy-done.6), kind=kOutput, calls=%fused_computation.1 | convolution fusion | flops 3233808384 | bytes 25362432 | tf_op jit(solution)/shard_map/kj,ijc->ikc/dot_general | solution.py:150
  197.4 11.2 copy.39
  208.7 90.2 %all-to-all-done = bf16[512,32,384]{2,1,0:T(8,128)(2,1)} async-done(((bf16[512,32,384]{2,1,0:T(8,128)(2,1)}), bf16[512,32,384]{2,1,0:T(8,128)(2,1)}, u32[]{:S(2)}, u32[]{:S(2)}) %all-to-all-start) | async-done | bytes 12582944 | tf_op jit(solution)/shard_map/all_to_all | solution.py:23
  298.9 0.0 all-gather.5.cloned.1.call-update
  298.9 0.0 copy-start.5
  298.9 84.3 %all-to-all-start.1 = ((bf16[512,32,384]{2,1,0:T(8,128)(2,1)}), bf16[512,32,384]{2,1,0:T(8,128)(2,1)}, u32[]{:S(2)}, u32[]{:S(2)}) async-start(bf16[512,32,384]{2,1,0:T(8,128)(2,1)} %bitcast.81), calls=%async_computation.1 | async-start | bytes 25165824 | tf_op jit(solution)/shard_map/all_to_all | solution.py:23
  383.2 0.2 all-gather.7.cloned.1.call-start
  383.4 1.1 copy.42
  384.5 0.0 all-gather.7.cloned.1.call-update
  384.5 34.4 %all-gather.5.cloned.1.call-done = bf16[1024,32,384]{2,1,0:T(8,128)(2,1)} async-done(((bf16[512,32,384]{2,1,0:T(8,128)(2,1)}), bf16[1024,32,384]{2,1,0:T(8,128)(2,1)}) %all-gather.5.cloned.1.call-update) | async-done | bytes 25165840 | tf_op jit(solution)/shard_map/all_gather | solution.py:158
  418.9 22.6 %copy.41 = bf16[1024,32,384]{2,0,1:T(8,128)(2,1)} copy(bf16[1024,32,384]{2,1,0:T(8,128)(2,1)} %all-gather.5.cloned.1.call-done) | data formatting | bytes 50331648 | tf_op jit(solution)/shard_map/all_gather | solution.py:158
  441.5 20.8 %bitcast_convert_fusion = bf16[512,32,384]{2,0,1:T(8,128)(2,1)} fusion(bf16[2,512,32,384]{3,1,0,2:T(8,128)(2,1)} %bitcast.84, bf16[768,2,384]{0,2,1:T(8,128)(2,1)} %bitcast.90, s32[]{:T(128)S(6)} %select_n.28), kind=kOutput, calls=%fused_computation | convolution fusion | flops 9669967872 | bytes 38338564 | tf_op jit(solution)/shard_map/hmkd,chd->mkc/dot_general | solution.py:159
  462.3 14.3 %convert_bitcast_fusion = bf16[512,32,384]{0,2,1:T(8,128)(2,1)} fusion(bf16[512,32,384]{2,0,1:T(8,128)(2,1)} %bitcast_convert_fusion, bf16[512,512]{1,0:T(8,128)(2,1)S(1)} %copy-done), kind=kOutput, calls=%fused_computation.7 | convolution fusion | flops 6448742400 | bytes 25690112 | tf_op jit(solution)/shard_map/mi,mkc->ikc/dot_general | solution.py:162
  476.7 181.3 %all-to-all-done.1 = bf16[512,32,384]{2,1,0:T(8,128)(2,1)} async-done(((bf16[512,32,384]{2,1,0:T(8,128)(2,1)}), bf16[512,32,384]{2,1,0:T(8,128)(2,1)}, u32[]{:S(2)}, u32[]{:S(2)}) %all-to-all-start.1) | async-done | bytes 12582944 | tf_op jit(solution)/shard_map/all_to_all | solution.py:23
  658.0 16.8 %copy.45 = bf16[512,32,384]{2,1,0:T(8,128)(2,1)} copy(bf16[512,32,384]{0,2,1:T(8,128)(2,1)} %convert_bitcast_fusion) | data formatting | bytes 25165824 | tf_op jit(solution)/shard_map/optimization_barrier | solution.py:165
  674.7 5.4 all-to-all-start.2
  680.1 0.3 all-reduce.8.cloned.1.call-start
  680.4 19.0 %fusion.16 = f32[512,512]{1,0:T(8,128)S(1)} fusion(bf16[512,32,384]{2,0,1:T(8,128)(2,1)} %bitcast_convert_fusion, bf16[512,32,384]{2,1,0:T(8,128)(2,1)} %all-to-all-done.1), kind=kOutput, calls=%fused_computation.13 | convolution fusion | flops 6442450944 | bytes 26214400 | tf_op jit(solution)/shard_map/mkc,ikc->mi/dot_general | solution.py:171
  699.4 0.0 slice-start
  699.4 0.1 collective-permute-start.3
  699.5 25.0 %fusion.11 = f32[2,384,384]{1,2,0:T(8,128)S(1)} fusion(bf16[2,512,32,384]{3,1,0,2:T(8,128)(2,1)} %bitcast.85, bf16[512,32,384]{2,1,0:T(8,128)(2,1)} %all-to-all-done.1, bf16[512,512]{1,0:T(8,128)(2,1)S(1)} %copy-done), kind=kOutput, calls=%fused_computation.12 | convolution fusion | flops 16112418816 | bytes 39452672 | tf_op jit(solution)/shard_map/mkc,hmkd->hcd/dot_general | solution.py:174
  724.5 0.0 copy-start.2
  724.5 0.9 dynamic-slice_bitcast_fusion.1
  725.4 0.5 collective-permute-start.2
  725.9 1.8 collective-permute-done.2
  727.7 1.1 maximum_select_fusion
  728.8 0.0 collective-permute-done.3
  728.8 2.4 add.85
  731.2 0.0 all-reduce.8.cloned.1.call-update
  731.3 0.0 all-reduce.6.cloned.1.call-start
  731.3 0.1 copy.47
  731.4 0.1 copy.46
  731.5 0.7 pad_convert_fusion.refs_4_
  732.2 0.7 maximum_convert_fusion.1
  732.9 250.5 %all-to-all-done.2 = bf16[512,32,384]{2,1,0:T(8,128)(2,1)} async-done(((bf16[512,32,384]{2,1,0:T(8,128)(2,1)}), bf16[512,32,384]{2,1,0:T(8,128)(2,1)}, u32[]{:S(2)}, u32[]{:S(2)}) %all-to-all-start.2) | async-done | bytes 12582944 | tf_op jit(solution)/shard_map/all_to_all | solution.py:23
  983.4 0.9 slice.140
  984.4 0.2 convolution_bitcast_fusion
  984.6 0.7 multiply_bitcast_fusion.2
  985.3 0.7 multiply_bitcast_fusion.1
  986.1 1.3 collective-permute-start.1
  987.4 51.1 %all-reduce.8.cloned.1.call-done = (f32[768,384]{1,0:T(8,128)}, f32[512,512]{1,0:T(8,128)}) async-done(((f32[768,384]{1,0:T(8,128)}, f32[512,512]{1,0:T(8,128)}), (f32[768,384]{1,0:T(8,128)}, f32[512,512]{1,0:T(8,128)})) %all-reduce.8.cloned.1.call-update) | async-done | bytes 2228240 | tf_op jit(solution)/shard_map/psum | solution.py:183
  1038.5 2.3 broadcast_multiply_fusion
  1040.8 91.7 %shard_map.110 = (bf16[16384,384]{1,0:T(8,128)(2,1)}, f32[256,256]{1,0:T(8,128)S(1)}, f32[2,4,8,384]{3,2,1,0:T(8,128)S(1)}) custom-call(bf16[8,64,32,384]{3,2,1,0:T(8,128)(2,1)} %bitcast.16.refs_0_, f32[256,64]{1,0:T(8,128)S(1)} %bitcast.77, bf16[16384,384]{1,0:T(8,128)(2,1)} %refs_3_.1, bf16[16384,384]{1,0:T(8,128)(2,1)} %refs_3_.1, ...), custom_call_target="tpu_custom_call" | custom-call | flops 6442450944 | bytes 50331648 | tf_op jit(solution)/shard_map/pallas_call | solution.py:98
  1132.6 0.1 copy.54
  1132.7 0.1 select_bitcast_fusion
  1132.8 0.7 pad_maximum_fusion
  1133.6 0.0 all-reduce.6.cloned.1.call-update
  1133.6 0.9 multiply_convert_fusion.2
  1134.5 88.3 %all-reduce.6.cloned.1.call-done = f32[71680]{0:T(1024)} async-done(((f32[71680]{0:T(1024)}), f32[71680]{0:T(1024)}) %all-reduce.6.cloned.1.call-update) | async-done | bytes 286736 | tf_op jit(solution)/shard_map/psum | solution.py:207
  1222.9 1.0 slice_multiply_fusion
  1223.8 0.8 mul.266
  1224.6 0.7 slice.146
  1225.4 0.6 multiply_bitcast_fusion
  (38 shorter events, 0.2 us)
Async XLA Ops:
  7.2 455.2 %copy-start = (bf16[512,512]{1,0:T(8,128)(2,1)S(1)}, bf16[512,512]{1,0:T(8,128)(2,1)}, u32[]{:S(2)}) copy-start(bf16[512,512]{1,0:T(8,128)(2,1)} %param.12) | copy-start | bytes 1572868
  18.4 12.6 %copy-start.1 = (f32[2,4,384]{2,1,0:T(4,128)S(1)}, f32[2,4,384]{2,1,0:T(4,128)}, u32[]{:S(2)}) copy-start(f32[2,4,384]{2,1,0:T(4,128)} %refs_6_.1) | copy-start | bytes 36868
  18.4 280.5 %all-to-all-start = ((bf16[512,32,384]{2,1,0:T(8,128)(2,1)}), bf16[512,32,384]{2,1,0:T(8,128)(2,1)}, u32[]{:S(2)}, u32[]{:S(2)}) async-start(bf16[512,32,384]{2,1,0:T(8,128)(2,1)} %bitcast.82), calls=%async_computation | async-start | bytes 25165824 | tf_op jit(solution)/shard_map/all_to_all | solution.py:23
  25.8 393.1 %all-gather.5.cloned.1.call-start = ((), (), s32[]{:S(2)}) async-start(), calls=%async_computation.4 | async-start | bytes 37748736 | tf_op jit(solution)/shard_map/all_gather | solution.py:158
  27.2 100.1 %collective-permute-start = (bf16[3,384]{1,0:T(4,128)(2,1)S(1)}, bf16[3,384]{1,0:T(4,128)(2,1)S(1)}, u32[]{:S(2)}, u32[]{:S(2)}) collective-permute-start(bf16[3,384]{1,0:T(4,128)(2,1)S(1)} %get-tuple-element.32), channel_id=1, source_target_pairs={{0,2},{2,4},{4,6},{6,8},{8,10},{10,12},{12,14},{1,3},{3,5},{5,7},{... | collective-permute-start | bytes 6920 | tf_op jit(solution)/shard_map/ppermute | solution.py:12
  31.1 110.3 %copy-start.8 = (f32[384]{0:T(512)}, f32[384]{0:T(512)S(1)}, u32[]{:S(2)}) copy-start(f32[384]{0:T(512)S(1)} %get-tuple-element.19) | copy-start | bytes 4612
  31.1 110.3 %copy-start.9 = (f32[384]{0:T(512)}, f32[384]{0:T(512)S(1)}, u32[]{:S(2)}) copy-start(f32[384]{0:T(512)S(1)} %get-tuple-element.23) | copy-start | bytes 4612
  31.1 110.3 %copy-start.10 = (f32[384]{0:T(512)}, f32[384]{0:T(512)S(1)}, u32[]{:S(2)}) copy-start(f32[384]{0:T(512)S(1)} %get-tuple-element.24) | copy-start | bytes 4612
  31.1 110.3 %copy-start.11 = (f32[384]{0:T(512)}, f32[384]{0:T(512)S(1)}, u32[]{:S(2)}) copy-start(f32[384]{0:T(512)S(1)} %get-tuple-element.25) | copy-start | bytes 4612
  31.1 110.3 %copy-start.12 = (f32[384]{0:T(512)}, f32[384]{0:T(512)S(1)}, u32[]{:S(2)}) copy-start(f32[384]{0:T(512)S(1)} %get-tuple-element.20) | copy-start | bytes 4612
  31.2 110.3 %copy-start.13 = (f32[384]{0:T(512)}, f32[384]{0:T(512)S(1)}, u32[]{:S(2)}) copy-start(f32[384]{0:T(512)S(1)} %get-tuple-element.21) | copy-start | bytes 4612
  31.2 110.3 %copy-start.14 = (f32[384]{0:T(512)}, f32[384]{0:T(512)S(1)}, u32[]{:S(2)}) copy-start(f32[384]{0:T(512)S(1)} %get-tuple-element.22) | copy-start | bytes 4612
  31.2 110.3 %copy-start.15 = (f32[384]{0:T(512)}, f32[384]{0:T(512)S(1)}, u32[]{:S(2)}) copy-start(f32[384]{0:T(512)S(1)} %get-tuple-element.26) | copy-start | bytes 4612
  127.2 14.2 %copy-start.7 = (bf16[3,384]{1,0:T(4,128)(2,1)}, bf16[3,384]{1,0:T(4,128)(2,1)S(1)}, u32[]{:S(2)}) copy-start(bf16[3,384]{1,0:T(4,128)(2,1)S(1)} %collective-permute-done) | copy-start | bytes 6916
  141.5 40.1 %copy-start.4 = (f32[64,256]{1,0:T(8,128)S(1)}, f32[64,256]{1,0:T(8,128)}, u32[]{:S(2)}) copy-start(f32[64,256]{1,0:T(8,128)} %param.11) | copy-start | bytes 196612
  141.5 40.1 %copy-start.6 = (bf16[256,256]{1,0:T(8,128)(2,1)S(1)}, bf16[256,256]{1,0:T(8,128)(2,1)}, u32[]{:S(2)}) copy-start(bf16[256,256]{1,0:T(8,128)(2,1)} %param.10) | copy-start | bytes 393220
  298.9 84.5 %copy-start.5 = (bf16[768,384]{1,0:T(8,128)(2,1)S(1)}, bf16[768,384]{1,0:T(8,128)(2,1)}, u32[]{:S(2)}) copy-start(bf16[768,384]{1,0:T(8,128)(2,1)} %param.13) | copy-start | bytes 1769476
  298.9 359.1 %all-to-all-start.1 = ((bf16[512,32,384]{2,1,0:T(8,128)(2,1)}), bf16[512,32,384]{2,1,0:T(8,128)(2,1)}, u32[]{:S(2)}, u32[]{:S(2)}) async-start(bf16[512,32,384]{2,1,0:T(8,128)(2,1)} %bitcast.81), calls=%async_computation.1 | async-start | bytes 25165824 | tf_op jit(solution)/shard_map/all_to_all | solution.py:23
  383.2 58.4 %all-gather.7.cloned.1.call-start = ((), (), s32[]{:S(2)}) async-start(), calls=%async_computation.5 | async-start | bytes 1769472 | tf_op jit(solution)/shard_map/all_gather | solution.py:142
  674.7 308.7 %all-to-all-start.2 = ((bf16[512,32,384]{2,1,0:T(8,128)(2,1)}), bf16[512,32,384]{2,1,0:T(8,128)(2,1)}, u32[]{:S(2)}, u32[]{:S(2)}) async-start(bf16[512,32,384]{2,1,0:T(8,128)(2,1)} %copy.45), calls=%async_computation.2 | async-start | bytes 25165824 | tf_op jit(solution)/shard_map/all_to_all | solution.py:23
  680.1 358.4 %all-reduce.8.cloned.1.call-start = ((), (), s32[]{:S(2)}) async-start(), calls=%async_computation.6 | async-start | bytes 4456448 | tf_op jit(solution)/shard_map/psum | solution.py:183
  699.4 285.0 %slice-start = ((f32[64,256]{1,0:T(8,128)}), f32[1,256]{1,0:T(1,128)S(1)}, s32[]{:S(2)}) async-start(f32[64,256]{1,0:T(8,128)} %param.11), calls=%async_computation.7 | async-start | bytes 2048 | tf_op jit(solution)/shard_map/slice | solution.py:191
  699.4 29.4 %collective-permute-start.3 = (f32[512,512]{1,0:T(8,128)S(1)}, f32[512,512]{1,0:T(8,128)}, u32[]{:S(2)}, u32[]{:S(2)}) collective-permute-start(f32[512,512]{1,0:T(8,128)S(1)} %fusion.16), channel_id=1, source_target_pairs={{0,1},{1,0},{2,3},{3,2},{4,5},{5,4},{6,7},{7,6},{8,9},{9,8},{10,11... | collective-permute-start | bytes 3145736 | tf_op jit(solution)/shard_map/ppermute | solution.py:179
  724.5 316.3 %copy-start.2 = (f32[2,4,384]{2,1,0:T(4,128)S(1)}, f32[2,4,384]{2,1,0:T(4,128)}, u32[]{:S(2)}) copy-start(f32[2,4,384]{2,1,0:T(4,128)} %refs_6_.1) | copy-start | bytes 36868
  725.4 2.3 collective-permute-start.2
  731.3 491.6 %all-reduce.6.cloned.1.call-start = ((), (), s32[]{:S(2)}) async-start(), calls=%async_computation.3 | async-start | bytes 573440 | tf_op jit(solution)/shard_map/psum | solution.py:207
  986.1 54.7 %collective-permute-start.1 = (f32[2,3,384]{2,1,0:T(4,128)S(1)}, f32[2,3,384]{2,1,0:T(4,128)S(1)}, u32[]{:S(2)}, u32[]{:S(2)}) collective-permute-start(f32[2,3,384]{2,1,0:T(4,128)S(1)} %pad_maximum_fusion.1), channel_id=1, source_target_pairs={{2,0},{4,2},{6,4},{8,6},{10,8},{12,10},{14,12},{3,1},{5,3},{7,5},{... | collective-permute-start | bytes 27656 | tf_op jit(solution)/shard_map/ppermute | solution.py:12
  1040.8 92.8 %copy-start.3 = (f32[768,384]{1,0:T(8,128)S(1)}, f32[768,384]{1,0:T(8,128)}, u32[]{:S(2)}) copy-start(f32[768,384]{1,0:T(8,128)} %get-tuple-element.27) | copy-start | bytes 3538948
Sparse Core Ops, SparseCore 0:
  299.0 119.8 all-gather.4
  421.0 10.3 all-gather.6
  731.4 307.0 all-reduce.7
  1133.7 89.0 all-reduce.5
